TPU v7x, 256 devices: a whole 4x4x8 slice. The times are simulated.
256 devices in a mesh: grp: 8 (over y_hi, x), blk: 32 (over y_lo, z, core).
Axes of the slice: x: 4, y: 4 (y_hi: 2, y_lo: 2; y = y_hi * 2 + y_lo), z: 8, core: 2. Of those that a mesh axis runs over, the one named last changes fastest.
Arguments:
- voltages: bfloat16 [4096, 188416], P(('blk', 'grp')), may hold values from -6 to 6
- filter_taps: float32 [8, 8192], replicated, may hold values from -0.0234375 to 0.0234375
- channel_index: int32 [16], replicated, may hold values from 0 to 4095
- antenna_slot_order: int32 [2048], replicated, may hold values from 0 to 2047, each once
Outputs:
- visibilities: bfloat16 [16, 4096, 2, 4096], P('grp', 'blk')
All inputs are finite; a program needn't handle non-finite values.
Results may differ from a plain program's by a relative error of at most 0.0065.
Values sent between devices are 32-bit elements; how exact they have to be, the bound alone decides.
A program may use at most 64 MiB of HBM per device.

v0:
```python
import math

import jax
import jax.numpy as jnp
from jax import lax
from jax.sharding import PartitionSpec as P


def in_order(tiles, dim):
    tiles = jnp.moveaxis(tiles, 0, dim)
    shape = tiles.shape
    return tiles.reshape(*shape[:dim], shape[dim] * shape[dim + 1], *shape[dim + 2 :])


def copy_for_each(array, axis):
    size = lax.axis_size(axis)
    return lax.all_to_all(
        jnp.broadcast_to(array[None], (size, *array.shape)), axis, 0, 0, tiled=True
    )


def gather_directly(array, axis, dim):
    return in_order(copy_for_each(array, axis), dim)


def phase_table(channel_index, fft_length):
    samples_idx = jnp.arange(fft_length, dtype=jnp.int32)
    phase = samples_idx[:, None] * channel_index[None, :] % fft_length
    angle = phase.astype(jnp.float32) * jnp.float32(2.0 * math.pi / fft_length)
    return jnp.concatenate([jnp.cos(angle), -jnp.sin(angle)], axis=1).astype(jnp.bfloat16)


def channelize(voltages, filter_taps, channel_index):
    tap_count, fft_length = filter_taps.shape
    row_count = voltages.shape[0]
    frame_count = voltages.shape[1] // fft_length
    spectra = frame_count - tap_count + 1
    blocked = voltages.reshape(row_count, frame_count, fft_length)
    filtered = jnp.zeros((row_count, spectra, fft_length), jnp.float32)
    for tap_index in range(tap_count):
        filtered = filtered + filter_taps[tap_index][None, None, :] * blocked[
            :, tap_index : tap_index + spectra, :
        ].astype(jnp.float32)
    twiddle = phase_table(channel_index, fft_length)
    spectrum = jnp.dot(
        filtered.astype(jnp.bfloat16).reshape(row_count * spectra, fft_length),
        twiddle,
        preferred_element_type=jnp.float32,
    )
    chan_count = channel_index.shape[0]
    return (
        spectrum.reshape(row_count, spectra, 2, chan_count)
        .transpose(3, 2, 1, 0)
        .reshape(chan_count, 2 * spectra, row_count)
    )


def column_index(antenna_slot_order):
    count = antenna_slot_order.shape[0]
    inverse = (
        jnp.zeros((count,), jnp.int32)
        .at[antenna_slot_order]
        .set(jnp.arange(count, dtype=jnp.int32))
    )
    column_entry = jnp.arange(2 * count, dtype=jnp.int32)
    return 2 * inverse[column_entry // 2] + column_entry % 2


def stacked_rows(block):
    half = block.shape[1] // 2
    turned = jnp.concatenate([block[:, half:], -block[:, :half]], axis=1)
    return jnp.stack([block, turned], axis=1)


def correlate(lhs, cols):
    return jnp.einsum(
        "cpkr,ckn->crpn",
        lhs,
        cols,
        precision=lax.Precision.HIGHEST,
        preferred_element_type=jnp.float32,
    )


def per_device(voltages, filter_taps, channel_index, antenna_slot_order):
    local = channelize(voltages, filter_taps, channel_index)
    scale = jnp.float32(1.0 / (local.shape[1] // 2))
    columns = column_index(antenna_slot_order)
    turned = lax.all_to_all(local, "grp", split_axis=0, concat_axis=2, tiled=True)
    lhs = stacked_rows(turned)
    everything = gather_directly(turned, "blk", 2)
    ordered = jnp.take(everything, columns, axis=2)
    result = (correlate(lhs, ordered) * scale).astype(jnp.bfloat16)
    return result


def solution(mesh):
    in_specs = (P(("blk", "grp"), None), P(), P(), P())
    out_specs = P("grp", "blk", None, None)
    return jax.shard_map(
        per_device, mesh=mesh, in_specs=in_specs, out_specs=out_specs, check_vma=False
    )
```

profile of v0, /device:TPU:1, one launch (start us, length us, event | category | flops | bytes accessed | tf_op | source)
XLA Modules:
  0.0 168.2 jit_solution(12724328822515265125)
XLA Ops:
  0.0 2.2 %fusion.21 = (f32[1,8192]{1,0:T(1,128)S(1)}, f32[1,8192]{1,0:T(1,128)S(1)}, f32[1,8192]{1,0:T(1,128)S(1)}, f32[1,8192]{1,0:T(1,128)S(1)}, f32[1,8192]{1,0:T(1,12...) fusion(f32[8,8192]{1,0:T(8,128)} %param.5), kind=kLoop, calls=%fused_computation.50 | loop fusion | bytes 524288 | tf_op jit(solution)/shard_map/slice | solution.py:41
  2.3 3.2 %cosine_convert_fusion = (bf16[8192,16]{0,1:T(8,128)(2,1)S(1)}, bf16[8192,16]{0,1:T(8,128)(2,1)S(1)}) fusion(s32[16]{0:T(128)} %param.6), kind=kLoop, calls=%fused_computation.18 | loop fusion | flops 2228224 | bytes 524352 | tf_op jit(solution)/shard_map/convert
  5.4 8.2 %reshape.112 = bf16[16,23,8192]{2,1,0:T(8,128)(2,1)} reshape(bf16[16,188416]{1,0:T(8,128)(2,1)} %param.4) | data formatting | bytes 12058624 | tf_op jit(solution)/shard_map/reshape | solution.py:38
  13.6 0.0 copy-start
  13.7 28.6 %fusion.1 = f32[16,16,2,16]{3,1,2,0:T(8,128)S(1)} fusion(bf16[2,16,8192,1]{2,1,0,3:T(8,128)(2,1)S(1)} %bitcast.49, bf16[16,23,8192]{2,1,0:T(8,128)(2,1)} %reshape.112, f32[8192]{0:T(1024)S(1)} %bitcast.60, f32[8192]{0:T(1024)S(1)} %bitcast.61, f32[8192]{0:T(1024)S(1)} %bitcast.55, f32[8192]{0:T(1024)S(1)} %bitcast.56, f32[8192]{0:T(1024)S(1)} %bitcast.57, ...), kind=kOutput, calls=%fused_computation.6 | convolution fusion | flops 184549376 | bytes 34373632 | tf_op jit(solution)/shard_map/dot_general | solution.py:45
  42.3 0.1 copy.17
  42.4 0.7 reshape.145
  43.1 7.5 %all-to-all-start = ((f32[8,1,1024]{2,1,0:T(1,128)}), f32[8,1,1024]{2,1,0:T(1,128)S(1)}, u32[]{:S(2)}, u32[]{:S(2)}) async-start(f32[8,1,1024]{2,1,0:T(1,128)} %reshape.145), calls=%async_computation | async-start | bytes 65536 | tf_op jit(solution)/shard_map/all_to_all | solution.py:89
  50.7 8.0 %scatter_custom_fusion = s32[2048]{0:T(1024)S(1)} fusion(s32[2048]{0:T(1024)S(1)} %compare_select_fusion.3, s32[2048]{0:T(1024)S(1)} %iota.16, s32[]{:T(128)} %constant.59.clone.1), kind=kCustom, calls=%fused_computation.47 | custom fusion | bytes 8196 | tf_op jit(solution)/shard_map/scatter | solution.py:63
  58.7 0.0 all-to-all-done
  58.7 0.5 broadcast.168
  59.2 0.7 reduce
  60.0 0.1 reshape.146
  60.1 0.1 copy.19
  60.1 1.1 broadcast_in_dim.27
  61.3 9.7 %all-to-all-start.1 = ((f32[32,2,32,128]{3,2,1,0:T(8,128)}), f32[32,2,32,128]{3,2,1,0:T(8,128)S(1)}, u32[]{:S(2)}, u32[]{:S(2)}) async-start(f32[32,2,32,128]{3,2,1,0:T(8,128)} %broadcast_in_dim.27), calls=%async_computation.1 | async-start | bytes 2097152 | tf_op jit(solution)/shard_map/all_to_all | solution.py:17
  71.0 23.0 %gather_fusion = s32[4096]{0:T(1024)S(1)} fusion(s32[2048]{0:T(1024)S(1)} %scatter_custom_fusion, s32[4096]{0:T(1024)S(1)} %broadcast_clamp_fusion.1), kind=kCustom, calls=%fused_computation | custom fusion | bytes 49152 | tf_op jit(solution)/shard_map/gather | solution.py:66
  94.1 0.1 copy.25
  94.2 3.2 %all-to-all-done.1 = f32[32,2,32,128]{3,2,1,0:T(8,128)S(1)} async-done(((f32[32,2,32,128]{3,2,1,0:T(8,128)}), f32[32,2,32,128]{3,2,1,0:T(8,128)S(1)}, u32[]{:S(2)}, u32[]{:S(2)}) %all-to-all-start.1) | async-done | bytes 1048608 | tf_op jit(solution)/shard_map/all_to_all | solution.py:17
  97.4 4.3 %copy.30 = f32[2,32,32,128]{1,0,3,2:T(2,128)} copy(f32[2,32,32,128]{3,1,0,2:T(8,128)S(1)} %bitcast.44) | data formatting | bytes 2097152 | tf_op jit(solution)/shard_map/reshape | solution.py:12
  101.7 30.4 %gather_fusion.1 = f32[4096,2,32]{2,1,0:T(2,128)} fusion(f32[2,32,4096]{1,0,2:T(2,128)} %bitcast.43, s32[4096]{0:T(1024)S(1)} %broadcast_clamp_fusion), kind=kCustom, calls=%fused_computation.1 | custom fusion | bytes 2113536 | tf_op jit(solution)/shard_map/jit(_take)/gather | solution.py:92
  132.1 16.3 %select_bitcast_fusion = f32[2,32,4096,1]{1,0,2,3:T(2,128)S(1)} fusion(f32[4096,2,32]{2,1,0:T(2,128)} %gather_fusion.1, pred[4096]{0:T(1024)(128)(4,1)S(1)} %compare_and_fusion), kind=kLoop, calls=%fused_computation.9 | loop fusion | flops 262144 | bytes 2101248 | tf_op jit(solution)/shard_map/jit(_take)/select_n | solution.py:92
  148.4 8.7 %fusion = bf16[2,128,2,4096]{1,3,2,0:T(8,128)(2,1)} fusion(f32[2,32,4096,1]{1,0,2,3:T(2,128)S(1)} %select_bitcast_fusion, f32[2,1,32,128]{3,2,1,0:T(8,128)S(1)} %maximum_bitcast_fusion, f32[2,1,32,128]{3,2,1,0:T(8,128)S(1)} %copy.25), kind=kOutput, calls=%fused_computation.5 | convolution fusion | flops 809517056 | bytes 5308416 | tf_op jit(solution)/shard_map/cpkr,ckn->crpn/dot_general | solution.py:76
  157.1 11.1 %copy.27 = bf16[2,128,2,4096]{3,2,1,0:T(2,128)(2,1)} copy(bf16[2,128,2,4096]{1,3,2,0:T(8,128)(2,1)} %fusion) | data formatting | bytes 8388608 | tf_op jit(solution)/shard_map/convert_element_type | solution.py:93
  (13 shorter events, 0.1 us)
Async XLA Ops:
  13.6 37.0 %copy-start = (s32[2048]{0:T(1024)S(1)}, s32[2048]{0:T(1024)}, u32[]{:S(2)}) copy-start(s32[2048]{0:T(1024)} %param.7) | copy-start | bytes 24580
  43.1 15.6 %all-to-all-start = ((f32[8,1,1024]{2,1,0:T(1,128)}), f32[8,1,1024]{2,1,0:T(1,128)S(1)}, u32[]{:S(2)}, u32[]{:S(2)}) async-start(f32[8,1,1024]{2,1,0:T(1,128)} %reshape.145), calls=%async_computation | async-start | bytes 65536 | tf_op jit(solution)/shard_map/all_to_all | solution.py:89
  61.3 36.1 %all-to-all-start.1 = ((f32[32,2,32,128]{3,2,1,0:T(8,128)}), f32[32,2,32,128]{3,2,1,0:T(8,128)S(1)}, u32[]{:S(2)}, u32[]{:S(2)}) async-start(f32[32,2,32,128]{3,2,1,0:T(8,128)} %broadcast_in_dim.27), calls=%async_computation.1 | async-start | bytes 2097152 | tf_op jit(solution)/shard_map/all_to_all | solution.py:17
where the time goes:
time: 171 us; the launch traced here: 168 us
  local copies, waits for them, and re-layouts  90.1 us (53%)
  matrix products  37.2 us (22%)
  other arithmetic  20.3 us (12%)
  starting transfers between devices  17.2 us (10%)
  waiting for transfers between devices  3.19 us (2%)
    gather x1, local copies, waits for them, and re-layouts, per_device(): ordered = jnp.take(everything, columns, axis=2)  30.4 us
    dot_general x1, matrix products, channelize(): jnp.dot(filtered.astype(jnp.bfloat16).reshape(row_count * spectra, fft_le...  28.6 us
    gather x1, local copies, waits for them, and re-layouts, column_index(): return 2 * inverse[column_entry // 2] + column_entry % 2  23 us
    select_n x2, other arithmetic, per_device(): ordered = jnp.take(everything, columns, axis=2)  16.4 us
    convert_element_type x1, local copies, waits for them, and re-layouts, per_device(): result = (correlate(lhs, ordered) * scale).astype(jnp.bfloat16)  11.1 us
    all_to_all x1, starting transfers between devices, copy_for_each(): lax.all_to_all(jnp.broadcast_to(array[None], (size, *array.shape)), axis,...  9.69 us
    dot_general x1, matrix products, correlate(): jnp.einsum('cpkr,ckn->crpn', lhs, cols, precision=lax.Precision.HIGHEST,...  8.65 us
    reshape x1, local copies, waits for them, and re-layouts, channelize(): blocked = voltages.reshape(row_count, frame_count, fft_length)  8.19 us
  transfers between devices with their start and end apart: 2, of which 1 were waited for; matrix products, arithmetic and copies ran while one was open for 19% of the time, Pallas kernels for 0%

commit v1 on v0

v1 whole, which is shorter than its diff:
```python
import functools
import math

import jax
import jax.numpy as jnp
from jax import lax
from jax.experimental import pallas as pl
from jax.experimental.pallas import tpu as pltpu
from jax.sharding import PartitionSpec as P

F32, BF16, I32 = jnp.float32, jnp.bfloat16, jnp.int32
MESH = pl.DeviceIdType.MESH
NFFT, TAPS, SPEC, FRAMES = 8192, 8, 16, 23
CHUNKS = 4
WIDTH = NFFT // CHUNKS
FORM = 1024
QBLOCK = 512


def iota(shape, dim):
    return lax.broadcasted_iota(I32, shape, dim)


def form_weights(index_ref, taps_ref, weights):
    shape = (32, 128)
    row, lane = iota(shape, 0), iota(shape, 1)
    channel = jnp.zeros(shape, I32)
    for c in range(16):
        channel = jnp.where(row >> 1 == c, index_ref[c], channel)
    real = (row & 1) == 0
    unit = jnp.float32(2.0 * math.pi / NFFT)
    fine = ((lane * channel) & (NFFT - 1)).astype(F32) * unit
    coarse = (((lane * channel) & 63) * 128).astype(F32) * unit
    cos_fine, sin_fine = jnp.cos(fine), jnp.sin(fine)
    cos_coarse, sin_coarse = jnp.cos(coarse), jnp.sin(coarse)
    first = jnp.where(real, cos_fine, -sin_fine)
    second = jnp.where(real, -sin_fine, -cos_fine)
    per = FORM // 128

    def step(i, _):
        shift = (128 - i * per) % 128
        cos_here = pltpu.roll(cos_coarse, shift, 1)
        sin_here = pltpu.roll(sin_coarse, shift, 1)
        for j in range(per):
            at = pl.ds(pl.multiple_of(i * FORM + j * 128, 128), 128)
            cos_b = jnp.broadcast_to(cos_here[:, j : j + 1], shape)
            sin_b = jnp.broadcast_to(sin_here[:, j : j + 1], shape)
            twiddle = (first * cos_b + second * sin_b).astype(BF16).astype(F32)
            for m in range(TAPS):
                weights[pl.ds(m * 32, 32), at] = (
                    taps_ref[pl.ds(m, 1), at] * twiddle
                ).astype(BF16)
        return _

    lax.fori_loop(0, NFFT // FORM, step, 0)


def channelize(index_ref, taps_ref, volts, volts_sem, weights, acc):
    form_weights(index_ref, taps_ref, weights)
    for c in range(CHUNKS):
        pltpu.make_async_copy(volts.at[c], volts.at[c], volts_sem.at[c]).wait()
        part = lax.dot_general(
            volts[c].reshape(FRAMES * 16, WIDTH),
            weights[:, pl.ds(c * WIDTH, WIDTH)],
            (((1,), (1,)), ((), ())),
            preferred_element_type=F32,
        )
        if c == 0:
            acc[...] = part
        else:
            acc[...] += part


def pieces_of(acc, pairs, pieces):
    lane = iota((16, 128), 1)
    group = lane >> 2
    sums = [
        acc[pl.ds(f * 16, 16), :128] + acc[pl.ds((f + 4) * 16, 16), 128:]
        for f in range(SPEC + 3)
    ]
    spectra = []
    for t in range(SPEC):
        x = sums[t + 3]
        for j in (2, 1, 0):
            x = jnp.where(lane < 32 * (j + 1), sums[t + j], x)
        x = x + pltpu.roll(x, 64, 1)
        spectra.append(x + pltpu.roll(x, 32, 1))
    turned = []
    for s in range(8):
        x = spectra[s]
        for q in range(1, 16):
            x = jnp.where((group & 15) == q, spectra[(q + s) % 16], x)
        turned.append(pltpu.roll(x, 4 * s, 1) if s else x)
    for g in range(8):
        x = turned[0]
        for s in range(1, 8):
            x = jnp.where(((group - g) & 7) == s, turned[s], x)
        pairs[g] = x
    low = iota((8, 128), 1) < 64
    for g in range(8):
        even = pairs[g, pl.ds(0, 8, stride=2), :]
        odd = pairs[g, pl.ds(1, 8, stride=2), :]
        pieces[g] = jnp.where(low, even, odd)


def spectra_kernel(
    index_ref, taps_ref, volts_hbm, out_ref,
    volts, weights, acc, pairs, pieces, buf,
    volts_sem, a_send, a_recv, z_send, z_recv, y_send, y_recv, c_send, c_recv,
):
    grp, blk = lax.axis_index("grp"), lax.axis_index("blk")
    yh, x = grp // 4, grp % 4
    yl, z, core = blk // 16, (blk // 2) % 8, blk % 2

    def start(c, _):
        for f in range(FRAMES):
            at = pl.ds(pl.multiple_of(f * NFFT + c * WIDTH, 128), WIDTH)
            pltpu.make_async_copy(
                volts_hbm.at[:, at], volts.at[c, f], volts_sem.at[c]
            ).start()
        return _

    lax.fori_loop(0, CHUNKS, start, 0)

    def at_grp(i, j):
        return ((yh + i) % 2 * 4 + (x + j) % 4, blk)

    def at_z(d):
        return (grp, (yl * 8 + (z + d) % 8) * 2 + core)

    others = [(i, j) for i in range(2) for j in range(4) if (i, j) != (0, 0)]
    y_device = (grp, ((1 - yl) * 8 + z) * 2 + core)
    c_device = (grp, blk + 1 - 2 * core)

    barrier = pltpu.get_barrier_semaphore()
    partners = [at_grp(i, j) for i, j in others] + [at_z(d) for d in range(1, 8)]
    partners += [y_device, c_device]
    for device in partners:
        pl.semaphore_signal(barrier, inc=1, device_id=device, device_id_type=MESH)

    channelize(index_ref, taps_ref, volts, volts_sem, weights, acc)
    pieces_of(acc, pairs, pieces)
    pl.semaphore_wait(barrier, len(partners))

    def send(src, dst, s, r, device):
        copy = pltpu.make_async_remote_copy(
            src_ref=src, dst_ref=dst, send_sem=s, recv_sem=r,
            device_id=device, device_id_type=MESH,
        )
        copy.start()
        sent.append(copy)

    sent = []
    for n, (i, j) in enumerate(sorted(others, key=lambda o: -2 * o[0] - min(o[1], 4 - o[1]))):
        device = at_grp(i, j)
        send(pieces.at[device[0]], buf.at[yl, z, core, grp], a_send.at[n], a_recv.at[n], device)
    buf[yl, z, core, grp] = pieces[grp]
    for copy in sent:
        copy.wait_recv()

    def level(y, d, c):
        return buf.at[y, (z - d + 8) % 8, c]

    arrivals = {}
    for d in (4, 3, 5, 2, 6, 1, 7):
        send(level(yl, 0, core), level(yl, 0, core), z_send.at[d], z_recv.at[d], at_z(d))
        arrivals["z", d] = sent[-1]
    order = (0, 1, 7, 2, 6, 3, 5, 4)

    def from_y(d):
        pltpu.make_async_copy(level(yl, d, core), level(yl, d, core), y_recv.at[d]).wait()
        here = level(1 - yl, d, core)
        send(here, here, c_send.at[8 + d], c_recv.at[8 + d], c_device)

    for n, d in enumerate(order):
        here = level(yl, d, core)
        if d:
            arrivals["z", d].wait_recv()
        send(here, here, y_send.at[d], y_recv.at[d], y_device)
        send(here, here, c_send.at[d], c_recv.at[d], c_device)
        if n >= 2:
            from_y(order[n - 2])
    for d in order[6:]:
        from_y(d)
    for d in range(16):
        here = level(yl, 0, core)
        pltpu.make_async_copy(here, here, c_recv.at[d]).wait()
    for copy in sent:
        copy.wait_send()
    out_ref[...] = buf[...].reshape(out_ref.shape)


def spectra_of_all(index, taps, volts):
    dma = pltpu.SemaphoreType.DMA
    vmem = pltpu.VMEM
    return pl.pallas_call(
        spectra_kernel,
        out_shape=jax.ShapeDtypeStruct((2048, 128), F32),
        in_specs=[
            pl.BlockSpec(memory_space=pltpu.SMEM),
            pl.BlockSpec(memory_space=pltpu.VMEM),
            pl.BlockSpec(memory_space=pl.ANY),
        ],
        out_specs=pl.BlockSpec(memory_space=pltpu.VMEM),
        scratch_shapes=[
            vmem((CHUNKS, FRAMES, 16, WIDTH), BF16),
            vmem((TAPS * 32, NFFT), BF16),
            vmem((FRAMES * 16, TAPS * 32), F32),
            vmem((8, 16, 128), F32),
            vmem((8, 8, 128), F32),
            vmem((2, 8, 2, 8, 8, 128), F32),
            dma((CHUNKS,)), dma((7,)), dma((7,)), dma((8,)), dma((8,)),
            dma((8,)), dma((8,)), dma((16,)), dma((16,)),
        ],
        compiler_params=pltpu.CompilerParams(
            collective_id=0, has_side_effects=True, vmem_limit_bytes=32 << 20
        ),
    )(index, taps, volts)


def prepare(order_ref, all_ref, onehot, permuted, rows, lhs, cols):
    lane = iota((128, 128), 1)

    def chunk(i, _):
        for half in range(2):
            r = i * 2 + half
            slots = order_ref[pl.ds(r, 1), :]
            wide = jnp.broadcast_to(slots.astype(F32), (128, 128)).T.astype(I32)
            for j in range(16):
                onehot[pl.ds(half * 128, 128), pl.ds(j * 128, 128)] = jnp.where(
                    wide == lane + j * 128, 1.0, 0.0
                ).astype(BF16)
        part = lax.dot_general(
            all_ref[pl.ds(pl.multiple_of(i * 256, 256), 256), :].astype(BF16),
            onehot[...],
            (((0,), (0,)), ((), ())),
            preferred_element_type=F32,
        )
        permuted[...] += part
        return _

    permuted[...] = jnp.zeros_like(permuted)
    lax.fori_loop(0, 8, chunk, 0)

    row, col = iota((256, 256), 0), iota((256, 256), 1)
    weave = jnp.where((col >> 1) + (col & 1) * 128 == row, 1.0, 0.0).astype(BF16)
    for j in range(16):
        at = pl.ds(j * 128, 128)
        both = jnp.concatenate([permuted[:64, at], permuted[64:, at]], axis=1)
        cols[:, pl.ds(j * 256, 256)] = jnp.dot(
            both.astype(BF16), weave, preferred_element_type=F32
        ).astype(BF16)

    blk = lax.axis_index("blk")
    mine = all_ref[pl.ds(pl.multiple_of(blk * 64, 64), 64), :] * jnp.float32(1.0 / SPEC)
    even = (iota((64, 128), 1) & 1) == 0
    crossed = jnp.where(even, pltpu.roll(mine, 127, 1), -pltpu.roll(mine, 1, 1))
    for o, part in enumerate((mine, crossed)):
        rows[pl.ds(o, 64, stride=4), :] = part
        rows[pl.ds(2 + o, 64, stride=4), :] = pltpu.roll(part, 64, 1)
    both = rows[...]
    channel = (iota(both.shape, 1) >> 1) & 1
    for c in range(2):
        lhs[c] = jnp.where(channel == c, both, 0.0).astype(BF16)[:, :64]


def correlate_kernel(order_ref, all_ref, out_ref, onehot, permuted, rows, lhs, cols):
    i = pl.program_id(0)

    @pl.when(i == 0)
    def _():
        prepare(order_ref, all_ref, onehot, permuted, rows, lhs, cols)

    right = cols[:, pl.ds(pl.multiple_of(i * QBLOCK, QBLOCK), QBLOCK)]
    for c in range(2):
        x = jnp.dot(lhs[c], right, preferred_element_type=F32)
        out_ref[c] = x.astype(BF16).reshape(128, 2, QBLOCK)


def correlate(order, spectra):
    vmem = pltpu.VMEM
    return pl.pallas_call(
        correlate_kernel,
        grid=(4096 // QBLOCK,),
        out_shape=jax.ShapeDtypeStruct((2, 128, 2, 4096), BF16),
        in_specs=[
            pl.BlockSpec((16, 128), lambda i: (0, 0)),
            pl.BlockSpec((2048, 128), lambda i: (0, 0)),
        ],
        out_specs=pl.BlockSpec((2, 128, 2, QBLOCK), lambda i: (0, 0, 0, i)),
        scratch_shapes=[
            vmem((256, 2048), BF16),
            vmem((128, 2048), F32),
            vmem((256, 128), F32),
            vmem((2, 256, 64), BF16),
            vmem((64, 4096), BF16),
        ],
        compiler_params=pltpu.CompilerParams(vmem_limit_bytes=32 << 20),
    )(order, spectra)


def per_device(voltages, filter_taps, channel_index, antenna_slot_order):
    spectra = spectra_of_all(channel_index, filter_taps, voltages)
    return correlate(antenna_slot_order.reshape(16, 128), spectra)


def solution(mesh):
    in_specs = (P(("blk", "grp"), None), P(), P(), P())
    out_specs = P("grp", "blk", None, None)
    return jax.shard_map(
        per_device, mesh=mesh, in_specs=in_specs, out_specs=out_specs, check_vma=False
    )
```

time: 171 us -> 56.5 us (0.33); the launches traced: 168 us -> 56.4 us
  local copies, waits for them, and re-layouts: 90.1 us -> 4.32 us
  Pallas kernels: 0 us -> 52 us
  matrix products: 37.2 us -> 0 us
  other arithmetic: 20.3 us -> 0 us
  starting transfers between devices: 17.2 us -> 0 us
  waiting for transfers between devices: 3.19 us -> 0 us
    gather x2 -> x0, local copies, waits for them, and re-layouts: 53.5 us -> none  [the longest x1 30.4 us: per_device(): ordered = jnp.take(everything, columns, axis=2)]
    pallas_call x0 -> x2, Pallas kernels: none -> 52 us  [the longest x1 41.4 us: spectra_of_all(): pl.pallas_call(spectra_kernel, out_shape=jax.ShapeDtypeStruct((2048, 128)...]
    dot_general x2 -> x0, matrix products: 37.2 us -> none  [the longest x1 28.6 us: channelize(): jnp.dot(filtered.astype(jnp.bfloat16).reshape(row_count * spectra, fft_le...]
    all_to_all x2 -> x0, starting transfers between devices: 17.2 us -> none  [the longest x1 9.69 us: copy_for_each(): lax.all_to_all(jnp.broadcast_to(array[None], (size, *array.shape)), axis,...]
    select_n x4 -> x0, other arithmetic: 16.4 us -> none  [the longest x2 16.4 us: per_device(): ordered = jnp.take(everything, columns, axis=2)]
    reshape x3 -> x0, local copies, waits for them, and re-layouts: 12.6 us -> none  [the longest x1 8.19 us: channelize(): blocked = voltages.reshape(row_count, frame_count, fft_length)]
    convert_element_type x1 -> x0, local copies, waits for them, and re-layouts: 11.1 us -> none  [per_device(): result = (correlate(lhs, ordered) * scale).astype(jnp.bfloat16)]
    scatter x1 -> x0, local copies, waits for them, and re-layouts: 8.05 us -> none  [column_index(): inverse = jnp.zeros((count,), jnp.int32).at[antenna_slot_order].set(jnp.a...]
  transfers between devices with their start and end apart: 2 -> 0, of which waited for: 1 -> 0; matrix products, arithmetic and copies ran while one was open for 19% -> 0% of each run, Pallas kernels for 0% -> 0%
where the time goes in v1:
time: 56.5 us; the launch traced here: 56.4 us
  Pallas kernels  52 us (92%)
  local copies, waits for them, and re-layouts  4.32 us (8%)
    pallas_call x1, Pallas kernels, spectra_of_all(): pl.pallas_call(spectra_kernel, out_shape=jax.ShapeDtypeStruct((2048, 128)...  41.4 us
    pallas_call x1, Pallas kernels, correlate(): pl.pallas_call(correlate_kernel, grid=(4096 // QBLOCK,), out_shape=jax.Sh...  10.7 us
    unnamed x8, local copies, waits for them, and re-layouts  4.32 us

profile of v1, /device:TPU:1, one launch (start us, length us, event | category | flops | bytes accessed | tf_op | source)
XLA Modules:
  0.0 56.4 jit_solution(6873911169249807245)
XLA Ops:
  0.0 0.0 copy-start
  0.0 2.7 %copy-done = bf16[16,188416]{1,0:T(8,128)(2,1)S(1)} copy-done((bf16[16,188416]{1,0:T(8,128)(2,1)S(1)}, bf16[16,188416]{1,0:T(8,128)(2,1)}, u32[]{:S(2)}) %copy-start) | copy-done | bytes 6029336
  2.7 0.0 copy-start.1
  2.7 0.9 %copy-done.1 = f32[8,8192]{1,0:T(8,128)S(1)} copy-done((f32[8,8192]{1,0:T(8,128)S(1)}, f32[8,8192]{1,0:T(8,128)}, u32[]{:S(2)}) %copy-start.1) | copy-done | bytes 262168
  3.7 0.0 copy-start.3
  3.7 0.7 %copy-done.3 = s32[16]{0:T(128)S(1)} copy-done((s32[16]{0:T(128)S(1)}, s32[16]{0:T(128)}, u32[]{:S(2)}) %copy-start.3) | copy-done | bytes 88
  4.3 0.0 copy-start.2
  4.3 41.4 %shard_map.46.all_ref = f32[2048,128]{1,0:T(8,128)S(1)} custom-call(s32[16]{0:T(128)S(1)} %copy-done.3, f32[8,8192]{1,0:T(8,128)S(1)} %copy-done.1, bf16[16,188416]{1,0:T(8,128)(2,1)S(1)} %copy-done), custom_call_target="tpu_custom_call" | custom-call | tf_op jit(solution)/shard_map/pallas_call | solution.py:196
  45.7 0.0 copy-done.2
  45.7 10.7 %shard_map.47 = bf16[2,128,2,4096]{3,2,1,0:T(2,128)(2,1)} custom-call(s32[16,128]{1,0:T(8,128)S(1)} %bitcast.1, f32[2048,128]{1,0:T(8,128)S(1)} %shard_map.46.all_ref), custom_call_target="tpu_custom_call" | custom-call | tf_op jit(solution)/shard_map/pallas_call | solution.py:282
Async XLA Ops:
  0.0 2.7 %copy-start = (bf16[16,188416]{1,0:T(8,128)(2,1)S(1)}, bf16[16,188416]{1,0:T(8,128)(2,1)}, u32[]{:S(2)}) copy-start(bf16[16,188416]{1,0:T(8,128)(2,1)} %volts_hbm.1) | copy-start | bytes 18087940
  2.7 0.9 %copy-start.1 = (f32[8,8192]{1,0:T(8,128)S(1)}, f32[8,8192]{1,0:T(8,128)}, u32[]{:S(2)}) copy-start(f32[8,8192]{1,0:T(8,128)} %taps_ref.1) | copy-start | bytes 786436
  3.7 0.7 %copy-start.3 = (s32[16]{0:T(128)S(1)}, s32[16]{0:T(128)}, u32[]{:S(2)}) copy-start(s32[16]{0:T(128)} %index_ref.1) | copy-start | bytes 196
  4.3 41.4 %copy-start.2 = (s32[2048]{0:T(1024)S(1)}, s32[2048]{0:T(1024)}, u32[]{:S(2)}) copy-start(s32[2048]{0:T(1024)} %param.7) | copy-start | bytes 24580

commit v2 on v1

v2 whole, which is shorter than its diff:
```python
import functools
import math

import jax
import jax.numpy as jnp
from jax import lax
from jax.experimental import pallas as pl
from jax.experimental.pallas import tpu as pltpu
from jax.sharding import PartitionSpec as P

F32, BF16, I32 = jnp.float32, jnp.bfloat16, jnp.int32
MESH = pl.DeviceIdType.MESH
NFFT, TAPS, SPEC, FRAMES = 8192, 8, 16, 23
WIDTH = 2048
FORM = 1024
QBLOCK = 512


def iota(shape, dim):
    return lax.broadcasted_iota(I32, shape, dim)


def form_weights(index_ref, taps_ref, weights):
    shape = (32, 128)
    row, lane = iota(shape, 0), iota(shape, 1)
    channel = jnp.zeros(shape, I32)
    for c in range(16):
        channel = jnp.where(row >> 1 == c, index_ref[c], channel)
    real = (row & 1) == 0
    unit = jnp.float32(2.0 * math.pi / NFFT)
    fine = ((lane * channel) & (NFFT - 1)).astype(F32) * unit
    coarse = (((lane * channel) & 63) * 128).astype(F32) * unit
    cos_fine, sin_fine = jnp.cos(fine), jnp.sin(fine)
    cos_coarse, sin_coarse = jnp.cos(coarse), jnp.sin(coarse)
    first = jnp.where(real, cos_fine, -sin_fine)
    second = jnp.where(real, -sin_fine, -cos_fine)
    per = FORM // 128

    def step(i, _):
        shift = (128 - i * per) % 128
        cos_here = pltpu.roll(cos_coarse, shift, 1)
        sin_here = pltpu.roll(sin_coarse, shift, 1)
        for j in range(per):
            at = pl.ds(pl.multiple_of(i * FORM + j * 128, 128), 128)
            cos_b = jnp.broadcast_to(cos_here[:, j : j + 1], shape)
            sin_b = jnp.broadcast_to(sin_here[:, j : j + 1], shape)
            twiddle = (first * cos_b + second * sin_b).astype(BF16).astype(F32)
            for m in range(TAPS):
                weights[pl.ds(m * 32, 32), at] = (
                    taps_ref[pl.ds(m, 1), at] * twiddle
                ).astype(BF16)
        return _

    lax.fori_loop(0, NFFT // FORM, step, 0)


def channelize(volts, weights, acc):
    for n in range(0, NFFT, WIDTH):
        part = lax.dot_general(
            volts[:, :, pl.ds(n, WIDTH)].reshape(FRAMES * 16, WIDTH),
            weights[:, pl.ds(n, WIDTH)],
            (((1,), (1,)), ((), ())),
            preferred_element_type=F32,
        )
        if n == 0:
            acc[...] = part
        else:
            acc[...] += part


def pieces_of(acc, pairs, pieces):
    lane = iota((16, 128), 1)
    group = lane >> 2
    sums = [
        acc[pl.ds(f * 16, 16), :128] + acc[pl.ds((f + 4) * 16, 16), 128:]
        for f in range(SPEC + 3)
    ]
    spectra = []
    for t in range(SPEC):
        x = sums[t + 3]
        for j in (2, 1, 0):
            x = jnp.where(lane < 32 * (j + 1), sums[t + j], x)
        x = x + pltpu.roll(x, 64, 1)
        spectra.append(x + pltpu.roll(x, 32, 1))
    turned = []
    for s in range(8):
        x = spectra[s]
        for q in range(1, 16):
            x = jnp.where((group & 15) == q, spectra[(q + s) % 16], x)
        turned.append(pltpu.roll(x, 4 * s, 1) if s else x)
    for g in range(8):
        x = turned[0]
        for s in range(1, 8):
            x = jnp.where(((group - g) & 7) == s, turned[s], x)
        pairs[g] = x
    low = iota((8, 128), 1) < 64
    for g in range(8):
        even = pairs[g, pl.ds(0, 8, stride=2), :]
        odd = pairs[g, pl.ds(1, 8, stride=2), :]
        pieces[g] = jnp.where(low, even, odd)


def form_onehot(order_ref, onehot):
    lane = iota((128, 128), 1)

    def step(r, _):
        slots = order_ref[pl.ds(r, 1), :].astype(F32)
        wide = jnp.broadcast_to(slots, (128, 128)).T.astype(I32)
        at = pl.ds(pl.multiple_of(r // 8 * 128, 128), 128)
        for j in range(16):
            onehot[r % 8, at, pl.ds(j * 128, 128)] = jnp.where(
                wide == lane + j * 128, 1.0, 0.0
            ).astype(BF16)
        return _

    lax.fori_loop(0, 16, step, 0)


def permute_level(buf, onehot, permuted, z, first):
    slots = jnp.concatenate(
        [buf[y, z].reshape(128, 128).astype(BF16) for y in range(2)], axis=0
    )
    part = lax.dot_general(
        slots, onehot[z], (((0,), (0,)), ((), ())), preferred_element_type=F32
    )
    if first:
        permuted[...] = part
    else:
        permuted[...] += part


def weave_columns(permuted, cols, cols_hbm, out_sem):
    row, col = iota((256, 256), 0), iota((256, 256), 1)
    weave = jnp.where((col >> 1) + (col & 1) * 128 == row, 1.0, 0.0).astype(BF16)
    for j in range(16):
        at = pl.ds(j * 128, 128)
        both = jnp.concatenate([permuted[:64, at], permuted[64:, at]], axis=1)
        cols[:, pl.ds(j * 256, 256)] = jnp.dot(
            both.astype(BF16), weave, preferred_element_type=F32
        ).astype(BF16)
        if j % 4 == 3:
            part = pl.ds((j - 3) * 256, 1024)
            pltpu.make_async_copy(cols.at[:, part], cols_hbm.at[:, part], out_sem).start()


def left_rows(mine, rows, lhs):
    mine = mine * jnp.float32(1.0 / SPEC)
    even = (iota((64, 128), 1) & 1) == 0
    crossed = jnp.where(even, pltpu.roll(mine, 127, 1), -pltpu.roll(mine, 1, 1))
    for o, part in enumerate((mine, crossed)):
        rows[pl.ds(o, 64, stride=4), :] = part
        rows[pl.ds(2 + o, 64, stride=4), :] = pltpu.roll(part, 64, 1)
    both = rows[...]
    channel = (iota(both.shape, 1) >> 1) & 1
    for c in range(2):
        lhs[pl.ds(c * 256, 256), :] = jnp.where(channel == c, both, 0.0).astype(BF16)[:, :64]


def hops(n, size):
    return min(n % size, -n % size)


def spectra_kernel(
    index_hbm, taps_hbm, order_hbm, volts_hbm, lhs_hbm, cols_hbm,
    index_ref, taps_ref, order_ref, volts, weights, acc, pairs, pieces, buf,
    onehot, permuted, rows, lhs, cols, in_sem, volts_sem, lhs_sem, cols_sem,
    s_send, s_recv, r_send, r_recv, y_send, y_recv, c_send, c_recv,
):
    grp, blk = lax.axis_index("grp"), lax.axis_index("blk")
    yh, x = grp // 4, grp % 4
    yl, z, core = blk // 16, (blk // 2) % 8, blk % 2

    inputs = [
        pltpu.make_async_copy(a, b, in_sem.at[n])
        for n, (a, b) in enumerate(
            [(index_hbm, index_ref), (taps_hbm, taps_ref), (order_hbm, order_ref)]
        )
    ]
    for copy in inputs:
        copy.start()
    for f in range(FRAMES):
        pltpu.make_async_copy(
            volts_hbm.at[:, pl.ds(f * NFFT, NFFT)], volts.at[f], volts_sem
        ).start()

    def device(i, j, d):
        return ((yh + i) % 2 * 4 + (x + j) % 4, (yl * 8 + (z + d + 8) % 8) * 2 + core)

    y_device = (grp, ((1 - yl) * 8 + z) * 2 + core)
    c_device = (grp, blk + 1 - 2 * core)
    direct = [
        (i, j, d) for i in range(2) for j in range(4) for d in (0, 1, 7, 2, 6)
        if (i, j, d) != (0, 0, 0)
    ]
    direct.sort(key=lambda m: (-hops(m[2], 8), -2 * m[0] - hops(m[1], 4)))

    barrier = pltpu.get_barrier_semaphore()
    partners = [device(*m) for m in direct] + [y_device, c_device]
    for to in partners:
        pl.semaphore_signal(barrier, inc=1, device_id=to, device_id_type=MESH)

    for copy in inputs:
        copy.wait()
    form_weights(index_ref, taps_ref, weights)
    pltpu.make_async_copy(volts, volts, volts_sem).wait()
    channelize(volts, weights, acc)
    pieces_of(acc, pairs, pieces)
    pl.semaphore_wait(barrier, len(partners))

    sent = []

    def send(ref, s, r, to, src=None):
        pltpu.make_async_remote_copy(
            src_ref=ref if src is None else src, dst_ref=ref, send_sem=s, recv_sem=r,
            device_id=to, device_id_type=MESH,
        ).start()
        if src is None:
            sent.append((ref, s))

    def wait(ref, sem):
        pltpu.make_async_copy(ref, ref, sem).wait()

    def level(y, d, c):
        return buf.at[y, (z - d + 8) % 8, c]

    own = buf.at[yl, z, core, grp]
    for m in direct:
        to = device(*m)
        send(own, s_send, s_recv.at[m[2]], to, src=pieces.at[to[0]])
    buf[yl, z, core, grp] = pieces[grp]
    form_onehot(order_ref, onehot)

    def forward(d):
        here = level(yl, d, core)
        send(here, y_send.at[d], y_recv.at[d], y_device)
        send(here, c_send.at[d], c_recv.at[d], c_device)

    def from_y(d):
        here = level(1 - yl, d, core)
        wait(here, y_recv.at[d])
        send(here, c_send.at[8 + d], c_recv.at[8 + d], c_device)

    done = []

    def permute(d):
        wait(level(yl, d, 1 - core), c_recv.at[d])
        wait(level(1 - yl, d, 1 - core), c_recv.at[8 + d])
        permute_level(buf, onehot, permuted, (z - d + 8) % 8, not done)
        done.append(d)

    half = [pl.ds(0, 4), pl.ds(4, 4)]
    far = (z + 4) % 8
    wait(level(yl, 1, core), s_recv.at[1])
    send(level(yl, 1, core), r_send.at[0], r_recv.at[0], device(0, 0, 2))
    wait(level(yl, 7, core), s_recv.at[7])
    send(level(yl, 7, core), r_send.at[1], r_recv.at[1], device(0, 0, 6))
    wait(level(yl, 2, core), s_recv.at[2])
    send(buf.at[yl, (z + 6) % 8, core, half[0]], r_send.at[2], r_recv.at[2], device(0, 0, 2))
    wait(level(yl, 6, core), s_recv.at[6])
    send(buf.at[yl, (z + 2) % 8, core, half[1]], r_send.at[3], r_recv.at[3], device(0, 0, 6))
    wait(buf.at[yl, z, core, pl.ds(0, 7)], s_recv.at[0])
    for d in (0, 1, 7, 2, 6):
        forward(d)
    for d in (0, 1, 7):
        from_y(d)
    wait(level(yl, 3, core), r_recv.at[0])
    forward(3)
    wait(level(yl, 5, core), r_recv.at[1])
    forward(5)
    from_y(2)
    for h in range(2):
        wait(buf.at[yl, far, core, half[h]], r_recv.at[2 + h])
    forward(4)
    from_y(6)
    permute(0)
    permute(1)
    from_y(3)
    permute(7)
    from_y(5)
    permute(2)
    from_y(4)
    for d in (6, 3, 5):
        permute(d)
    left_rows(buf[pl.ds(yl, 1), pl.ds(z, 1), pl.ds(core, 1)].reshape(64, 128), rows, lhs)
    pltpu.make_async_copy(lhs, lhs_hbm, lhs_sem).start()
    permute(4)
    weave_columns(permuted, cols, cols_hbm, cols_sem)
    for ref, s in sent:
        wait(ref, s)
    for n in range(len(direct) // 8):
        wait(buf.at[0, 0, 0], s_send)
    wait(buf.at[0, 0, 0, pl.ds(0, len(direct) % 8)], s_send)
    wait(lhs, lhs_sem)
    wait(cols, cols_sem)


def spectra_of_all(index, taps, order, volts):
    dma = pltpu.SemaphoreType.DMA
    vmem = pltpu.VMEM
    return pl.pallas_call(
        spectra_kernel,
        out_shape=[
            jax.ShapeDtypeStruct((512, 64), BF16),
            jax.ShapeDtypeStruct((64, 4096), BF16),
        ],
        in_specs=[pl.BlockSpec(memory_space=pltpu.HBM)] * 4,
        out_specs=[pl.BlockSpec(memory_space=pltpu.HBM)] * 2,
        scratch_shapes=[
            pltpu.SMEM((16,), I32),
            vmem((TAPS, NFFT), F32),
            vmem((16, 128), I32),
            vmem((FRAMES, 16, NFFT), BF16),
            vmem((TAPS * 32, NFFT), BF16),
            vmem((FRAMES * 16, TAPS * 32), F32),
            vmem((8, 16, 128), F32),
            vmem((8, 8, 128), F32),
            vmem((2, 8, 2, 8, 8, 128), F32),
            vmem((8, 256, 2048), BF16),
            vmem((128, 2048), F32),
            vmem((256, 128), F32),
            vmem((512, 64), BF16),
            vmem((64, 4096), BF16),
            dma((3,)), dma, dma, dma,
            dma, dma((8,)), dma((4,)), dma((4,)),
            dma((8,)), dma((8,)), dma((16,)), dma((16,)),
        ],
        compiler_params=pltpu.CompilerParams(
            collective_id=0, has_side_effects=True, vmem_limit_bytes=63 << 20
        ),
    )(index, taps, order, volts)


def correlate_kernel(lhs_ref, cols_ref, out_ref):
    x = jnp.dot(lhs_ref[...], cols_ref[...], preferred_element_type=F32)
    out_ref[...] = x.astype(BF16).reshape(2, 128, 2, QBLOCK)


def correlate(lhs, cols):
    return pl.pallas_call(
        correlate_kernel,
        grid=(4096 // QBLOCK,),
        out_shape=jax.ShapeDtypeStruct((2, 128, 2, 4096), BF16),
        in_specs=[
            pl.BlockSpec((512, 64), lambda i: (0, 0)),
            pl.BlockSpec((64, QBLOCK), lambda i: (0, i)),
        ],
        out_specs=pl.BlockSpec((2, 128, 2, QBLOCK), lambda i: (0, 0, 0, i)),
        compiler_params=pltpu.CompilerParams(vmem_limit_bytes=63 << 20),
    )(lhs, cols)


def per_device(voltages, filter_taps, channel_index, antenna_slot_order):
    lhs, cols = spectra_of_all(
        channel_index, filter_taps, antenna_slot_order.reshape(16, 128), voltages
    )
    return correlate(lhs, cols)


def solution(mesh):
    in_specs = (P(("blk", "grp"), None), P(), P(), P())
    out_specs = P("grp", "blk", None, None)
    return jax.shard_map(
        per_device, mesh=mesh, in_specs=in_specs, out_specs=out_specs, check_vma=False
    )
```

time: 56.5 us -> 40.9 us (0.72)
  Pallas kernels: 52 us -> 40.5 us
  local copies, waits for them, and re-layouts: 4.32 us -> 0 us
    pallas_call x1, Pallas kernels: 41.4 us -> 34.1 us  [spectra_of_all(): pl.pallas_call(spectra_kernel, out_shape=[jax.ShapeDtypeStruct((512, 64),...]
    unnamed x8 -> x0, local copies, waits for them, and re-layouts: 4.32 us -> none
    pallas_call x1, Pallas kernels: 10.7 us -> 6.45 us  [correlate(): pl.pallas_call(correlate_kernel, grid=(4096 // QBLOCK,), out_shape=jax.Sh...]
where the time goes in v2:
time: 40.9 us; the launch traced here: 40.5 us
  Pallas kernels  40.5 us (99%)
    pallas_call x1, Pallas kernels, spectra_of_all(): pl.pallas_call(spectra_kernel, out_shape=[jax.ShapeDtypeStruct((512, 64),...  34.1 us
    pallas_call x1, Pallas kernels, correlate(): pl.pallas_call(correlate_kernel, grid=(4096 // QBLOCK,), out_shape=jax.Sh...  6.45 us

profile of v2, /device:TPU:1, one launch (start us, length us, event | category | flops | bytes accessed | tf_op | source)
XLA Modules:
  0.0 40.5 jit_solution(66359310812995232)
XLA Ops:
  0.0 34.1 %shard_map.46 = (bf16[512,64]{1,0:T(8,128)(2,1)}, bf16[64,4096]{1,0:T(8,128)(2,1)}) custom-call(s32[16]{0:T(128)} %index_hbm.1, f32[8,8192]{1,0:T(8,128)} %taps_hbm.1, s32[16,128]{1,0:T(8,128)} %bitcast.1, bf16[16,188416]{1,0:T(8,128)(2,1)} %volts_hbm.1), custom_call_target="tpu_custom_call" | custom-call | tf_op jit(solution)/shard_map/pallas_call | solution.py:300
  34.1 6.5 %shard_map.47 = bf16[2,128,2,4096]{3,2,1,0:T(2,128)(2,1)} custom-call(bf16[512,64]{1,0:T(8,128)(2,1)} %get-tuple-element.7.lhs_ref, bf16[64,4096]{1,0:T(8,128)(2,1)} %get-tuple-element.8.cols_ref), custom_call_target="tpu_custom_call" | custom-call | tf_op jit(solution)/shard_map/pallas_call | solution.py:339

commit v3 on v2

--- a/solution.py
+++ b/solution.py
@@ -13,7 +13,8 @@
 NFFT, TAPS, SPEC, FRAMES = 8192, 8, 16, 23
 WIDTH = 2048
 FORM = 1024
-QBLOCK = 512
+QBLOCK = 1024
+PLACE = {0: 0, 1: 1, 7: 2, 2: 3, 6: 4, 3: 5, 5: 6, 4: 7}
 
 
 def iota(shape, dim):
@@ -116,9 +117,10 @@
     lax.fori_loop(0, 16, step, 0)
 
 
-def permute_level(buf, onehot, permuted, z, first):
+def permute_level(buf, place, onehot, permuted, z, first):
     slots = jnp.concatenate(
-        [buf[y, z].reshape(128, 128).astype(BF16) for y in range(2)], axis=0
+        [buf[y, c, place].reshape(64, 128).astype(BF16) for y in range(2) for c in range(2)],
+        axis=0,
     )
     part = lax.dot_general(
         slots, onehot[z], (((0,), (0,)), ((), ())), preferred_element_type=F32
@@ -164,11 +166,11 @@
     index_hbm, taps_hbm, order_hbm, volts_hbm, lhs_hbm, cols_hbm,
     index_ref, taps_ref, order_ref, volts, weights, acc, pairs, pieces, buf,
     onehot, permuted, rows, lhs, cols, in_sem, volts_sem, lhs_sem, cols_sem,
-    s_send, s_recv, r_send, r_recv, y_send, y_recv, c_send, c_recv,
+    s_send, s_recv, t_recv, r_send, r_recv, y_send, y_recv, c_send, c_recv,
 ):
     grp, blk = lax.axis_index("grp"), lax.axis_index("blk")
-    yh, x = grp // 4, grp % 4
-    yl, z, core = blk // 16, (blk // 2) % 8, blk % 2
+    yh, x = grp // 4, lax.rem(grp, 4)
+    yl, z, core = blk // 16, lax.rem(blk // 2, 8), lax.rem(blk, 2)
 
     inputs = [
         pltpu.make_async_copy(a, b, in_sem.at[n])
@@ -183,19 +185,21 @@
             volts_hbm.at[:, pl.ds(f * NFFT, NFFT)], volts.at[f], volts_sem
         ).start()
 
-    def device(i, j, d):
-        return ((yh + i) % 2 * 4 + (x + j) % 4, (yl * 8 + (z + d + 8) % 8) * 2 + core)
-
-    y_device = (grp, ((1 - yl) * 8 + z) * 2 + core)
+    def device(i, j, d, f=0):
+        return (
+            lax.rem(yh + i, 2) * 4 + lax.rem(x + j, 4),
+            (lax.rem(yl + f, 2) * 8 + lax.rem(z + d, 8)) * 2 + core,
+        )
+
     c_device = (grp, blk + 1 - 2 * core)
-    direct = [
-        (i, j, d) for i in range(2) for j in range(4) for d in (0, 1, 7, 2, 6)
-        if (i, j, d) != (0, 0, 0)
-    ]
-    direct.sort(key=lambda m: (-hops(m[2], 8), -2 * m[0] - hops(m[1], 4)))
+    near = (0, 1, 7)
+    direct = [(i, j, d, 0) for i in range(2) for j in range(4) for d in near + (2, 6)]
+    direct += [(i, j, d, 1) for i in range(2) for j in range(4) for d in near]
+    direct.remove((0, 0, 0, 0))
+    direct.sort(key=lambda m: (m[3], -hops(m[2], 8), -2 * m[0] - hops(m[1], 4)))
 
     barrier = pltpu.get_barrier_semaphore()
-    partners = [device(*m) for m in direct] + [y_device, c_device]
+    partners = [device(*m) for m in direct] + [c_device]
     for to in partners:
         pl.semaphore_signal(barrier, inc=1, device_id=to, device_id_type=MESH)
 
@@ -209,80 +213,91 @@
 
     sent = []
 
-    def send(ref, s, r, to, src=None):
+    def send(src, s, r, to, dst=None):
+        dst = src if dst is None else dst
         pltpu.make_async_remote_copy(
-            src_ref=ref if src is None else src, dst_ref=ref, send_sem=s, recv_sem=r,
+            src_ref=src, dst_ref=dst, send_sem=s, recv_sem=r,
             device_id=to, device_id_type=MESH,
         ).start()
-        if src is None:
-            sent.append((ref, s))
+        sent.append((src, s))
 
     def wait(ref, sem):
         pltpu.make_async_copy(ref, ref, sem).wait()
 
-    def level(y, d, c):
-        return buf.at[y, (z - d + 8) % 8, c]
-
-    own = buf.at[yl, z, core, grp]
+    def held(y, first, count=1):
+        return buf.at[y, core, pl.ds(first, count)]
+
     for m in direct:
         to = device(*m)
-        send(own, s_send, s_recv.at[m[2]], to, src=pieces.at[to[0]])
-    buf[yl, z, core, grp] = pieces[grp]
+        pltpu.make_async_remote_copy(
+            src_ref=pieces.at[to[0]], dst_ref=buf.at[yl, core, PLACE[m[2]], grp],
+            send_sem=s_send, recv_sem=(t_recv if m[3] else s_recv).at[m[2]],
+            device_id=to, device_id_type=MESH,
+        ).start()
+    buf[yl, core, 0, grp] = pieces[grp]
     form_onehot(order_ref, onehot)
 
-    def forward(d):
-        here = level(yl, d, core)
-        send(here, y_send.at[d], y_recv.at[d], y_device)
-        send(here, c_send.at[d], c_recv.at[d], c_device)
-
-    def from_y(d):
-        here = level(1 - yl, d, core)
-        wait(here, y_recv.at[d])
-        send(here, c_send.at[8 + d], c_recv.at[8 + d], c_device)
-
-    done = []
+    y_device = device(0, 0, 0, 1)
+    up, down = device(0, 0, 2), device(0, 0, 6)
+
+    def to_y(n, first, count):
+        send(held(yl, first, count), y_send.at[n], y_recv.at[n], y_device)
+
+    def to_core(n, y, first, count):
+        send(held(y, first, count), c_send.at[n], c_recv.at[n], c_device)
+
+    def from_core(n, y, first, count):
+        wait(buf.at[y, 1 - core, pl.ds(first, count)], c_recv.at[n])
 
     def permute(d):
-        wait(level(yl, d, 1 - core), c_recv.at[d])
-        wait(level(1 - yl, d, 1 - core), c_recv.at[8 + d])
-        permute_level(buf, onehot, permuted, (z - d + 8) % 8, not done)
-        done.append(d)
-
-    half = [pl.ds(0, 4), pl.ds(4, 4)]
-    far = (z + 4) % 8
-    wait(level(yl, 1, core), s_recv.at[1])
-    send(level(yl, 1, core), r_send.at[0], r_recv.at[0], device(0, 0, 2))
-    wait(level(yl, 7, core), s_recv.at[7])
-    send(level(yl, 7, core), r_send.at[1], r_recv.at[1], device(0, 0, 6))
-    wait(level(yl, 2, core), s_recv.at[2])
-    send(buf.at[yl, (z + 6) % 8, core, half[0]], r_send.at[2], r_recv.at[2], device(0, 0, 2))
-    wait(level(yl, 6, core), s_recv.at[6])
-    send(buf.at[yl, (z + 2) % 8, core, half[1]], r_send.at[3], r_recv.at[3], device(0, 0, 6))
-    wait(buf.at[yl, z, core, pl.ds(0, 7)], s_recv.at[0])
-    for d in (0, 1, 7, 2, 6):
-        forward(d)
-    for d in (0, 1, 7):
-        from_y(d)
-    wait(level(yl, 3, core), r_recv.at[0])
-    forward(3)
-    wait(level(yl, 5, core), r_recv.at[1])
-    forward(5)
-    from_y(2)
+        permute_level(buf, PLACE[d], onehot, permuted, lax.rem(z - d + 8, 8), d == 0)
+
+    def half(place, h):
+        return buf.at[yl, core, place, pl.ds(4 * h, 4)]
+
+    wait(held(yl, 1), s_recv.at[1])
+    send(held(yl, 1), r_send.at[0], r_recv.at[0], up, held(yl, 5))
+    wait(held(yl, 2), s_recv.at[7])
+    send(held(yl, 2), r_send.at[1], r_recv.at[1], down, held(yl, 6))
+    wait(held(yl, 3), s_recv.at[2])
+    send(half(3, 0), r_send.at[2], r_recv.at[2], up, half(7, 0))
+    wait(held(yl, 4), s_recv.at[6])
+    send(half(4, 1), r_send.at[3], r_recv.at[3], down, half(7, 1))
+    to_y(0, 3, 2)
+    wait(buf.at[yl, core, 0, pl.ds(0, 7)], s_recv.at[0])
+    to_core(0, yl, 0, 5)
+    for d in near:
+        wait(held(1 - yl, PLACE[d]), t_recv.at[d])
+    to_core(1, 1 - yl, 0, 3)
+    wait(held(yl, 5), r_recv.at[0])
+    wait(held(yl, 6), r_recv.at[1])
+    to_y(1, 5, 2)
+    to_core(2, yl, 5, 2)
+    wait(held(1 - yl, 3, 2), y_recv.at[0])
+    to_core(3, 1 - yl, 3, 2)
     for h in range(2):
-        wait(buf.at[yl, far, core, half[h]], r_recv.at[2 + h])
-    forward(4)
-    from_y(6)
-    permute(0)
-    permute(1)
-    from_y(3)
-    permute(7)
-    from_y(5)
+        wait(half(7, h), r_recv.at[2 + h])
+    to_y(2, 7, 1)
+    to_core(4, yl, 7, 1)
+    from_core(0, yl, 0, 5)
+    from_core(1, 1 - yl, 0, 3)
+    for d in near:
+        permute(d)
+    wait(held(1 - yl, 5, 2), y_recv.at[1])
+    to_core(5, 1 - yl, 5, 2)
+    from_core(3, 1 - yl, 3, 2)
     permute(2)
-    from_y(4)
-    for d in (6, 3, 5):
-        permute(d)
-    left_rows(buf[pl.ds(yl, 1), pl.ds(z, 1), pl.ds(core, 1)].reshape(64, 128), rows, lhs)
+    permute(6)
+    wait(held(1 - yl, 7), y_recv.at[2])
+    to_core(6, 1 - yl, 7, 1)
+    from_core(2, yl, 5, 2)
+    from_core(5, 1 - yl, 5, 2)
+    permute(3)
+    permute(5)
+    left_rows(buf[pl.ds(yl, 1), pl.ds(core, 1), pl.ds(0, 1)].reshape(64, 128), rows, lhs)
     pltpu.make_async_copy(lhs, lhs_hbm, lhs_sem).start()
+    from_core(4, yl, 7, 1)
+    from_core(6, 1 - yl, 7, 1)
     permute(4)
     weave_columns(permuted, cols, cols_hbm, cols_sem)
     for ref, s in sent:
@@ -314,15 +329,15 @@
             vmem((FRAMES * 16, TAPS * 32), F32),
             vmem((8, 16, 128), F32),
             vmem((8, 8, 128), F32),
-            vmem((2, 8, 2, 8, 8, 128), F32),
+            vmem((2, 2, 8, 8, 8, 128), F32),
             vmem((8, 256, 2048), BF16),
             vmem((128, 2048), F32),
             vmem((256, 128), F32),
             vmem((512, 64), BF16),
             vmem((64, 4096), BF16),
             dma((3,)), dma, dma, dma,
-            dma, dma((8,)), dma((4,)), dma((4,)),
-            dma((8,)), dma((8,)), dma((16,)), dma((16,)),
+            dma, dma((8,)), dma((8,)), dma((4,)), dma((4,)),
+            dma((3,)), dma((3,)), dma((7,)), dma((7,)),
         ],
         compiler_params=pltpu.CompilerParams(
             collective_id=0, has_side_effects=True, vmem_limit_bytes=63 << 20
@@ -330,21 +345,40 @@
     )(index, taps, order, volts)
 
 
-def correlate_kernel(lhs_ref, cols_ref, out_ref):
-    x = jnp.dot(lhs_ref[...], cols_ref[...], preferred_element_type=F32)
-    out_ref[...] = x.astype(BF16).reshape(2, 128, 2, QBLOCK)
+def correlate_kernel(lhs_hbm, cols_hbm, out_hbm, lhs, cols, out, lhs_sem, cols_sem, out_sem):
+    steps = 4096 // QBLOCK
+    left = pltpu.make_async_copy(lhs_hbm, lhs, lhs_sem)
+    left.start()
+    right = []
+    for i in range(steps):
+        at = pl.ds(i * QBLOCK, QBLOCK)
+        right.append(pltpu.make_async_copy(cols_hbm.at[:, at], cols.at[:, at], cols_sem.at[i]))
+        right[i].start()
+    left.wait()
+    for i in range(steps):
+        at = pl.ds(i * QBLOCK, QBLOCK)
+        right[i].wait()
+        for c in range(2):
+            x = jnp.dot(lhs[pl.ds(c * 256, 256), :], cols[:, at], preferred_element_type=F32)
+            out[i, c] = x.astype(BF16).reshape(128, 2, QBLOCK)
+        pltpu.make_async_copy(out.at[i], out_hbm.at[:, :, :, at], out_sem).start()
+    pltpu.make_async_copy(out, out, out_sem).wait()
 
 
 def correlate(lhs, cols):
+    dma = pltpu.SemaphoreType.DMA
+    vmem = pltpu.VMEM
     return pl.pallas_call(
         correlate_kernel,
-        grid=(4096 // QBLOCK,),
         out_shape=jax.ShapeDtypeStruct((2, 128, 2, 4096), BF16),
-        in_specs=[
-            pl.BlockSpec((512, 64), lambda i: (0, 0)),
-            pl.BlockSpec((64, QBLOCK), lambda i: (0, i)),
+        in_specs=[pl.BlockSpec(memory_space=pltpu.HBM)] * 2,
+        out_specs=pl.BlockSpec(memory_space=pltpu.HBM),
+        scratch_shapes=[
+            vmem((512, 64), BF16),
+            vmem((64, 4096), BF16),
+            vmem((4096 // QBLOCK, 2, 128, 2, QBLOCK), BF16),
+            dma, dma((4096 // QBLOCK,)), dma,
         ],
-        out_specs=pl.BlockSpec((2, 128, 2, QBLOCK), lambda i: (0, 0, 0, i)),
         compiler_params=pltpu.CompilerParams(vmem_limit_bytes=63 << 20),
     )(lhs, cols)
 

time: 40.9 us -> 37.4 us (0.914)
  Pallas kernels: 40.5 us -> 37.3 us
    pallas_call x1, Pallas kernels: 6.45 us -> 3.83 us  [correlate(): pl.pallas_call(correlate_kernel, out_shape=jax.ShapeDtypeStruct((2, 128,...]
    pallas_call x1, Pallas kernels: 34.1 us -> 33.5 us  [spectra_of_all(): pl.pallas_call(spectra_kernel, out_shape=[jax.ShapeDtypeStruct((512, 64),...]
where the time goes in v3:
time: 37.4 us; the launch traced here: 37.3 us
  Pallas kernels  37.3 us (100%)
    pallas_call x1, Pallas kernels, spectra_of_all(): pl.pallas_call(spectra_kernel, out_shape=[jax.ShapeDtypeStruct((512, 64),...  33.5 us
    pallas_call x1, Pallas kernels, correlate(): pl.pallas_call(correlate_kernel, out_shape=jax.ShapeDtypeStruct((2, 128,...  3.83 us

profile of v3, /device:TPU:1, one launch (start us, length us, event | category | flops | bytes accessed | tf_op | source)
XLA Modules:
  0.0 37.3 jit_solution(12976211948771678153)
XLA Ops:
  0.0 33.5 %shard_map.46 = (bf16[512,64]{1,0:T(8,128)(2,1)}, bf16[64,4096]{1,0:T(8,128)(2,1)}) custom-call(s32[16]{0:T(128)} %index_hbm.1, f32[8,8192]{1,0:T(8,128)} %taps_hbm.1, s32[16,128]{1,0:T(8,128)} %bitcast.1, bf16[16,188416]{1,0:T(8,128)(2,1)} %volts_hbm.1), custom_call_target="tpu_custom_call" | custom-call | tf_op jit(solution)/shard_map/pallas_call | solution.py:315
  33.5 3.8 %shard_map.47 = bf16[2,128,2,4096]{3,2,1,0:T(2,128)(2,1)} custom-call(bf16[512,64]{1,0:T(8,128)(2,1)} %get-tuple-element.7.lhs_hbm, bf16[64,4096]{1,0:T(8,128)(2,1)} %get-tuple-element.8.cols_hbm), custom_call_target="tpu_custom_call" | custom-call | tf_op jit(solution)/shard_map/pallas_call | solution.py:371

commit v4 on v3

--- a/solution.py
+++ b/solution.py
@@ -11,7 +11,7 @@
 F32, BF16, I32 = jnp.float32, jnp.bfloat16, jnp.int32
 MESH = pl.DeviceIdType.MESH
 NFFT, TAPS, SPEC, FRAMES = 8192, 8, 16, 23
-WIDTH = 2048
+GROUPS = ((0, 12), (12, 11))
 FORM = 1024
 QBLOCK = 1024
 PLACE = {0: 0, 1: 1, 7: 2, 2: 3, 6: 4, 3: 5, 5: 6, 4: 7}
@@ -21,52 +21,55 @@
     return lax.broadcasted_iota(I32, shape, dim)
 
 
-def form_weights(index_ref, taps_ref, weights):
+def cos_turns(phase):
+    phase = phase & (NFFT - 1)
+    fold = jnp.where(phase > NFFT // 2, NFFT - phase, phase)
+    x = (NFFT // 4 - fold).astype(F32) * jnp.float32(2.0 * math.pi / NFFT)
+    square = x * x
+    total = jnp.full(x.shape, 1.0 / math.factorial(13), F32)
+    for n in (11, 9, 7, 5, 3, 1):
+        total = total * square + jnp.float32((-1) ** (n // 2) / math.factorial(n))
+    return total * x
+
+
+def tables(index_ref):
     shape = (32, 128)
     row, lane = iota(shape, 0), iota(shape, 1)
     channel = jnp.zeros(shape, I32)
     for c in range(16):
         channel = jnp.where(row >> 1 == c, index_ref[c], channel)
-    real = (row & 1) == 0
-    unit = jnp.float32(2.0 * math.pi / NFFT)
-    fine = ((lane * channel) & (NFFT - 1)).astype(F32) * unit
-    coarse = (((lane * channel) & 63) * 128).astype(F32) * unit
-    cos_fine, sin_fine = jnp.cos(fine), jnp.sin(fine)
-    cos_coarse, sin_coarse = jnp.cos(coarse), jnp.sin(coarse)
-    first = jnp.where(real, cos_fine, -sin_fine)
-    second = jnp.where(real, -sin_fine, -cos_fine)
-    per = FORM // 128
-
-    def step(i, _):
-        shift = (128 - i * per) % 128
-        cos_here = pltpu.roll(cos_coarse, shift, 1)
-        sin_here = pltpu.roll(sin_coarse, shift, 1)
-        for j in range(per):
-            at = pl.ds(pl.multiple_of(i * FORM + j * 128, 128), 128)
-            cos_b = jnp.broadcast_to(cos_here[:, j : j + 1], shape)
-            sin_b = jnp.broadcast_to(sin_here[:, j : j + 1], shape)
-            twiddle = (first * cos_b + second * sin_b).astype(BF16).astype(F32)
-            for m in range(TAPS):
-                weights[pl.ds(m * 32, 32), at] = (
-                    taps_ref[pl.ds(m, 1), at] * twiddle
-                ).astype(BF16)
-        return _
-
-    lax.fori_loop(0, NFFT // FORM, step, 0)
-
-
-def channelize(volts, weights, acc):
-    for n in range(0, NFFT, WIDTH):
-        part = lax.dot_general(
-            volts[:, :, pl.ds(n, WIDTH)].reshape(FRAMES * 16, WIDTH),
-            weights[:, pl.ds(n, WIDTH)],
+    quarter = NFFT // 4
+    fine = lane * channel + (row & 1) * quarter
+    coarse = (lane & 63) * channel * 128 - (lane >> 6) * quarter
+    return cos_turns(fine), cos_turns(fine + quarter), cos_turns(coarse)
+
+
+def form_weights(factors, taps_ref, weights):
+    first, second, coarse = factors
+    for block in range(NFFT // 128):
+        cos_b = jnp.broadcast_to(coarse[:, block : block + 1], first.shape)
+        sin_b = jnp.broadcast_to(coarse[:, 64 + block : 65 + block], first.shape)
+        twiddle = (first * cos_b + second * sin_b).astype(BF16).astype(F32)
+        at = pl.ds(block * 128 % FORM, 128)
+        for m in range(TAPS):
+            weights[block * 128 // FORM][pl.ds(m * 32, 32), at] = (
+                taps_ref[pl.ds(m, 1), pl.ds(block * 128, 128)] * twiddle
+            ).astype(BF16)
+
+
+def channelize(volts, weights, acc, first, count):
+    at = pl.ds(first * 16, count * 16)
+    for n, part in enumerate(weights):
+        x = lax.dot_general(
+            volts[pl.ds(first, count), :, pl.ds(n * FORM, FORM)].reshape(count * 16, FORM),
+            part[...],
             (((1,), (1,)), ((), ())),
             preferred_element_type=F32,
         )
         if n == 0:
-            acc[...] = part
+            acc[at, :] = x
         else:
-            acc[...] += part
+            acc[at, :] += x
 
 
 def pieces_of(acc, pairs, pieces):
@@ -164,9 +167,9 @@
 
 def spectra_kernel(
     index_hbm, taps_hbm, order_hbm, volts_hbm, lhs_hbm, cols_hbm,
-    index_ref, taps_ref, order_ref, volts, weights, acc, pairs, pieces, buf,
+    index_ref, taps_ref, order_ref, volts, acc, pairs, pieces, buf,
     onehot, permuted, rows, lhs, cols, in_sem, volts_sem, lhs_sem, cols_sem,
-    s_send, s_recv, t_recv, r_send, r_recv, y_send, y_recv, c_send, c_recv,
+    s_send, s_recv, t_recv, r_send, r_recv, y_send, y_recv, c_send, c_recv, *weights,
 ):
     grp, blk = lax.axis_index("grp"), lax.axis_index("blk")
     yh, x = grp // 4, lax.rem(grp, 4)
@@ -178,12 +181,13 @@
             [(index_hbm, index_ref), (taps_hbm, taps_ref), (order_hbm, order_ref)]
         )
     ]
-    for copy in inputs:
+    for copy in inputs[:2]:
         copy.start()
-    for f in range(FRAMES):
-        pltpu.make_async_copy(
-            volts_hbm.at[:, pl.ds(f * NFFT, NFFT)], volts.at[f], volts_sem
-        ).start()
+    for n, (first, count) in enumerate(GROUPS):
+        for f in range(first, first + count):
+            pltpu.make_async_copy(
+                volts_hbm.at[:, pl.ds(f * NFFT, NFFT)], volts.at[f], volts_sem.at[n]
+            ).start(priority=f % 2)
 
     def device(i, j, d, f=0):
         return (
@@ -203,11 +207,15 @@
     for to in partners:
         pl.semaphore_signal(barrier, inc=1, device_id=to, device_id_type=MESH)
 
-    for copy in inputs:
-        copy.wait()
-    form_weights(index_ref, taps_ref, weights)
-    pltpu.make_async_copy(volts, volts, volts_sem).wait()
-    channelize(volts, weights, acc)
+    inputs[2].start()
+    inputs[0].wait()
+    factors = tables(index_ref)
+    inputs[1].wait()
+    form_weights(factors, taps_ref, weights)
+    for n, (first, count) in enumerate(GROUPS):
+        part = volts.at[pl.ds(first, count)]
+        pltpu.make_async_copy(part, part, volts_sem.at[n]).wait()
+        channelize(volts, weights, acc, first, count)
     pieces_of(acc, pairs, pieces)
     pl.semaphore_wait(barrier, len(partners))
 
@@ -235,6 +243,7 @@
             device_id=to, device_id_type=MESH,
         ).start()
     buf[yl, core, 0, grp] = pieces[grp]
+    inputs[2].wait()
     form_onehot(order_ref, onehot)
 
     y_device = device(0, 0, 0, 1)
@@ -325,7 +334,6 @@
             vmem((TAPS, NFFT), F32),
             vmem((16, 128), I32),
             vmem((FRAMES, 16, NFFT), BF16),
-            vmem((TAPS * 32, NFFT), BF16),
             vmem((FRAMES * 16, TAPS * 32), F32),
             vmem((8, 16, 128), F32),
             vmem((8, 8, 128), F32),
@@ -335,9 +343,10 @@
             vmem((256, 128), F32),
             vmem((512, 64), BF16),
             vmem((64, 4096), BF16),
-            dma((3,)), dma, dma, dma,
+            dma((3,)), dma((len(GROUPS),)), dma, dma,
             dma, dma((8,)), dma((8,)), dma((4,)), dma((4,)),
             dma((3,)), dma((3,)), dma((7,)), dma((7,)),
+            *[vmem((TAPS * 32, FORM), BF16)] * (NFFT // FORM),
         ],
         compiler_params=pltpu.CompilerParams(
             collective_id=0, has_side_effects=True, vmem_limit_bytes=63 << 20

time: 37.4 us -> 36.4 us (0.973)
  Pallas kernels: 37.3 us -> 36.3 us
    pallas_call x1, Pallas kernels: 33.5 us -> 32.5 us  [spectra_of_all(): pl.pallas_call(spectra_kernel, out_shape=[jax.ShapeDtypeStruct((512, 64),...]
where the time goes in v4:
time: 36.4 us; the launch traced here: 36.3 us
  Pallas kernels  36.3 us (100%)
    pallas_call x1, Pallas kernels, spectra_of_all(): pl.pallas_call(spectra_kernel, out_shape=[jax.ShapeDtypeStruct((512, 64),...  32.5 us
    pallas_call x1, Pallas kernels, correlate(): pl.pallas_call(correlate_kernel, out_shape=jax.ShapeDtypeStruct((2, 128,...  3.81 us

profile of v4, /device:TPU:1, one launch (start us, length us, event | category | flops | bytes accessed | tf_op | source)
XLA Modules:
  0.0 36.3 jit_solution(17763434367461094993)
XLA Ops:
  0.0 32.5 %shard_map.46 = (bf16[512,64]{1,0:T(8,128)(2,1)}, bf16[64,4096]{1,0:T(8,128)(2,1)}) custom-call(s32[16]{0:T(128)} %index_hbm.1, f32[8,8192]{1,0:T(8,128)} %taps_hbm.1, s32[16,128]{1,0:T(8,128)} %bitcast.1, bf16[16,188416]{1,0:T(8,128)(2,1)} %volts_hbm.1), custom_call_target="tpu_custom_call" | custom-call | tf_op jit(solution)/shard_map/pallas_call | solution.py:324
  32.5 3.8 %shard_map.47 = bf16[2,128,2,4096]{3,2,1,0:T(2,128)(2,1)} custom-call(bf16[512,64]{1,0:T(8,128)(2,1)} %get-tuple-element.7.lhs_hbm, bf16[64,4096]{1,0:T(8,128)(2,1)} %get-tuple-element.8.cols_hbm), custom_call_target="tpu_custom_call" | custom-call | tf_op jit(solution)/shard_map/pallas_call | solution.py:380

commit v5 on v4

--- a/solution.py
+++ b/solution.py
@@ -197,13 +197,15 @@
 
     c_device = (grp, blk + 1 - 2 * core)
     near = (0, 1, 7)
-    direct = [(i, j, d, 0) for i in range(2) for j in range(4) for d in near + (2, 6)]
-    direct += [(i, j, d, 1) for i in range(2) for j in range(4) for d in near]
+    direct = [
+        (i, j, d, f) for i in range(2) for j in range(4) for d in near for f in range(2)
+    ]
     direct.remove((0, 0, 0, 0))
-    direct.sort(key=lambda m: (m[3], -hops(m[2], 8), -2 * m[0] - hops(m[1], 4)))
+    direct.sort(key=lambda m: (-hops(m[2], 8), m[3], -2 * m[0] - hops(m[1], 4)))
 
     barrier = pltpu.get_barrier_semaphore()
-    partners = [device(*m) for m in direct] + [c_device]
+    partners = [device(*m) for m in direct] + [device(0, 0, d) for d in (2, 3, 5, 6)]
+    partners.append(c_device)
     for to in partners:
         pl.semaphore_signal(barrier, inc=1, device_id=to, device_id_type=MESH)
 
@@ -247,7 +249,7 @@
     form_onehot(order_ref, onehot)
 
     y_device = device(0, 0, 0, 1)
-    up, down = device(0, 0, 2), device(0, 0, 6)
+    other = 1 - yl
 
     def to_y(n, first, count):
         send(held(yl, first, count), y_send.at[n], y_recv.at[n], y_device)
@@ -261,52 +263,62 @@
     def permute(d):
         permute_level(buf, PLACE[d], onehot, permuted, lax.rem(z - d + 8, 8), d == 0)
 
-    def half(place, h):
-        return buf.at[yl, core, place, pl.ds(4 * h, 4)]
-
-    wait(held(yl, 1), s_recv.at[1])
-    send(held(yl, 1), r_send.at[0], r_recv.at[0], up, held(yl, 5))
-    wait(held(yl, 2), s_recv.at[7])
-    send(held(yl, 2), r_send.at[1], r_recv.at[1], down, held(yl, 6))
-    wait(held(yl, 3), s_recv.at[2])
-    send(half(3, 0), r_send.at[2], r_recv.at[2], up, half(7, 0))
-    wait(held(yl, 4), s_recv.at[6])
-    send(half(4, 1), r_send.at[3], r_recv.at[3], down, half(7, 1))
+    def half(y, place, h):
+        return buf.at[y, core, place, pl.ds(4 * h, 4)]
+
+    def relay(h, y, o, steps):
+        for n in steps:
+            n_sem, to = 3 * h + n - 1, device(0, 0, n if h == 0 else 8 - n)
+            if n == 3:
+                src, dst = half(y, 1 + h, h), half(y, 7, h)
+            else:
+                src, dst = held(y, 1 + h), held(y, 1 + h + 2 * n)
+            send(src, r_send.at[o, n_sem], r_recv.at[o, n_sem], to, dst)
+
+    def relayed(y, o, n):
+        for h in range(2):
+            dst = half(y, 7, h) if n == 3 else held(y, 1 + h + 2 * n)
+            wait(dst, r_recv.at[o, 3 * h + n - 1])
+
+    for h, d in enumerate((1, 7)):
+        wait(held(yl, 1 + h), s_recv.at[d])
+        relay(h, yl, 0, (1, 3, 2))
+    for h, d in enumerate((1, 7)):
+        wait(held(other, 1 + h), t_recv.at[d])
+        relay(h, other, 1, (3, 2))
+    wait(buf.at[yl, core, 0, pl.ds(0, 7)], s_recv.at[0])
+    to_core(0, yl, 0, 3)
+    wait(held(other, 0), t_recv.at[0])
+    to_core(1, other, 0, 3)
+    relayed(yl, 0, 1)
     to_y(0, 3, 2)
-    wait(buf.at[yl, core, 0, pl.ds(0, 7)], s_recv.at[0])
-    to_core(0, yl, 0, 5)
-    for d in near:
-        wait(held(1 - yl, PLACE[d]), t_recv.at[d])
-    to_core(1, 1 - yl, 0, 3)
-    wait(held(yl, 5), r_recv.at[0])
-    wait(held(yl, 6), r_recv.at[1])
-    to_y(1, 5, 2)
-    to_core(2, yl, 5, 2)
-    wait(held(1 - yl, 3, 2), y_recv.at[0])
-    to_core(3, 1 - yl, 3, 2)
-    for h in range(2):
-        wait(half(7, h), r_recv.at[2 + h])
-    to_y(2, 7, 1)
-    to_core(4, yl, 7, 1)
-    from_core(0, yl, 0, 5)
-    from_core(1, 1 - yl, 0, 3)
+    to_core(2, yl, 3, 2)
+    from_core(0, yl, 0, 3)
+    from_core(1, other, 0, 3)
     for d in near:
         permute(d)
-    wait(held(1 - yl, 5, 2), y_recv.at[1])
-    to_core(5, 1 - yl, 5, 2)
-    from_core(3, 1 - yl, 3, 2)
+    left_rows(buf[pl.ds(yl, 1), pl.ds(core, 1), pl.ds(0, 1)].reshape(64, 128), rows, lhs)
+    pltpu.make_async_copy(lhs, lhs_hbm, lhs_sem).start()
+    relayed(yl, 0, 2)
+    to_core(3, yl, 5, 2)
+    wait(held(other, 3, 2), y_recv.at[0])
+    to_core(4, other, 3, 2)
+    relayed(yl, 0, 3)
+    to_core(5, yl, 7, 1)
+    relayed(other, 1, 2)
+    to_core(6, other, 5, 2)
+    relayed(other, 1, 3)
+    to_core(7, other, 7, 1)
+    from_core(2, yl, 3, 2)
+    from_core(4, other, 3, 2)
     permute(2)
     permute(6)
-    wait(held(1 - yl, 7), y_recv.at[2])
-    to_core(6, 1 - yl, 7, 1)
-    from_core(2, yl, 5, 2)
-    from_core(5, 1 - yl, 5, 2)
+    from_core(3, yl, 5, 2)
+    from_core(6, other, 5, 2)
     permute(3)
     permute(5)
-    left_rows(buf[pl.ds(yl, 1), pl.ds(core, 1), pl.ds(0, 1)].reshape(64, 128), rows, lhs)
-    pltpu.make_async_copy(lhs, lhs_hbm, lhs_sem).start()
-    from_core(4, yl, 7, 1)
-    from_core(6, 1 - yl, 7, 1)
+    from_core(5, yl, 7, 1)
+    from_core(7, other, 7, 1)
     permute(4)
     weave_columns(permuted, cols, cols_hbm, cols_sem)
     for ref, s in sent:
@@ -344,8 +356,8 @@
             vmem((512, 64), BF16),
             vmem((64, 4096), BF16),
             dma((3,)), dma((len(GROUPS),)), dma, dma,
-            dma, dma((8,)), dma((8,)), dma((4,)), dma((4,)),
-            dma((3,)), dma((3,)), dma((7,)), dma((7,)),
+            dma, dma((8,)), dma((8,)), dma((2, 6)), dma((2, 6)),
+            dma((1,)), dma((1,)), dma((8,)), dma((8,)),
             *[vmem((TAPS * 32, FORM), BF16)] * (NFFT // FORM),
         ],
         compiler_params=pltpu.CompilerParams(

time: 36.4 us -> 36.3 us (level)
  no operation moved by 1% of the time
where the time goes in v5:
time: 36.3 us; the launch traced here: 36.2 us
  Pallas kernels  36.2 us (100%)
    pallas_call x1, Pallas kernels, spectra_of_all(): pl.pallas_call(spectra_kernel, out_shape=[jax.ShapeDtypeStruct((512, 64),...  32.4 us
    pallas_call x1, Pallas kernels, correlate(): pl.pallas_call(correlate_kernel, out_shape=jax.ShapeDtypeStruct((2, 128,...  3.82 us

profile of v5, /device:TPU:1, one launch (start us, length us, event | category | flops | bytes accessed | tf_op | source)
XLA Modules:
  0.0 36.2 jit_solution(5480806670141693702)
XLA Ops:
  0.0 32.4 %shard_map.46 = (bf16[512,64]{1,0:T(8,128)(2,1)}, bf16[64,4096]{1,0:T(8,128)(2,1)}) custom-call(s32[16]{0:T(128)} %index_hbm.1, f32[8,8192]{1,0:T(8,128)} %taps_hbm.1, s32[16,128]{1,0:T(8,128)} %bitcast.1, bf16[16,188416]{1,0:T(8,128)(2,1)} %volts_hbm.1), custom_call_target="tpu_custom_call" | custom-call | tf_op jit(solution)/shard_map/pallas_call | solution.py:336
  32.4 3.8 %shard_map.47 = bf16[2,128,2,4096]{3,2,1,0:T(2,128)(2,1)} custom-call(bf16[512,64]{1,0:T(8,128)(2,1)} %get-tuple-element.7.lhs_hbm, bf16[64,4096]{1,0:T(8,128)(2,1)} %get-tuple-element.8.cols_hbm), custom_call_target="tpu_custom_call" | custom-call | tf_op jit(solution)/shard_map/pallas_call | solution.py:392

commit v6 on v5

--- a/solution.py
+++ b/solution.py
@@ -201,7 +201,7 @@
         (i, j, d, f) for i in range(2) for j in range(4) for d in near for f in range(2)
     ]
     direct.remove((0, 0, 0, 0))
-    direct.sort(key=lambda m: (-hops(m[2], 8), m[3], -2 * m[0] - hops(m[1], 4)))
+    direct.sort(key=lambda m: (-hops(m[2], 8), hops(2 * m[0] + m[3], 4) + hops(m[1], 4)))
 
     barrier = pltpu.get_barrier_semaphore()
     partners = [device(*m) for m in direct] + [device(0, 0, d) for d in (2, 3, 5, 6)]
@@ -241,7 +241,7 @@
         to = device(*m)
         pltpu.make_async_remote_copy(
             src_ref=pieces.at[to[0]], dst_ref=buf.at[yl, core, PLACE[m[2]], grp],
-            send_sem=s_send, recv_sem=(t_recv if m[3] else s_recv).at[m[2]],
+            send_sem=s_send, recv_sem=(t_recv if m[3] else s_recv).at[m[0] if m[2] else 0, m[2]],
             device_id=to, device_id_type=MESH,
         ).start()
     buf[yl, core, 0, grp] = pieces[grp]
@@ -263,32 +263,31 @@
     def permute(d):
         permute_level(buf, PLACE[d], onehot, permuted, lax.rem(z - d + 8, 8), d == 0)
 
-    def half(y, place, h):
-        return buf.at[y, core, place, pl.ds(4 * h, 4)]
-
-    def relay(h, y, o, steps):
+    def some(y, place, i, n, h):
+        row = 4 * lax.rem(yh + i, 2)
+        return buf.at[y, core, place, pl.ds(row + 2 * h, 2) if n == 3 else pl.ds(row, 4)]
+
+    def relay(h, y, o, i, steps):
         for n in steps:
-            n_sem, to = 3 * h + n - 1, device(0, 0, n if h == 0 else 8 - n)
-            if n == 3:
-                src, dst = half(y, 1 + h, h), half(y, 7, h)
-            else:
-                src, dst = held(y, 1 + h), held(y, 1 + h + 2 * n)
-            send(src, r_send.at[o, n_sem], r_recv.at[o, n_sem], to, dst)
+            sem, to = 3 * h + n - 1, device(0, 0, n if h == 0 else 8 - n)
+            src = some(y, 1 + h, i, n, h)
+            dst = some(y, 7 if n == 3 else 1 + h + 2 * n, i, n, h)
+            send(src, r_send.at[o, i, sem], r_recv.at[o, i, sem], to, dst)
 
     def relayed(y, o, n):
-        for h in range(2):
-            dst = half(y, 7, h) if n == 3 else held(y, 1 + h + 2 * n)
-            wait(dst, r_recv.at[o, 3 * h + n - 1])
-
-    for h, d in enumerate((1, 7)):
-        wait(held(yl, 1 + h), s_recv.at[d])
-        relay(h, yl, 0, (1, 3, 2))
-    for h, d in enumerate((1, 7)):
-        wait(held(other, 1 + h), t_recv.at[d])
-        relay(h, other, 1, (3, 2))
-    wait(buf.at[yl, core, 0, pl.ds(0, 7)], s_recv.at[0])
+        for i in range(2):
+            for h in range(2):
+                dst = some(y, 7 if n == 3 else 1 + h + 2 * n, i, n, h)
+                wait(dst, r_recv.at[o, i, 3 * h + n - 1])
+
+    for o, i in ((0, 0), (1, 0), (1, 1), (0, 1)):
+        y = other if o else yl
+        for h, d in enumerate((1, 7)):
+            wait(some(y, 1 + h, i, 0, h), (t_recv if o else s_recv).at[i, d])
+            relay(h, y, o, i, (3, 2) if o else (1, 3, 2))
+    wait(buf.at[yl, core, 0, pl.ds(0, 7)], s_recv.at[0, 0])
     to_core(0, yl, 0, 3)
-    wait(held(other, 0), t_recv.at[0])
+    wait(held(other, 0), t_recv.at[0, 0])
     to_core(1, other, 0, 3)
     relayed(yl, 0, 1)
     to_y(0, 3, 2)
@@ -356,7 +355,7 @@
             vmem((512, 64), BF16),
             vmem((64, 4096), BF16),
             dma((3,)), dma((len(GROUPS),)), dma, dma,
-            dma, dma((8,)), dma((8,)), dma((2, 6)), dma((2, 6)),
+            dma, dma((2, 8)), dma((2, 8)), dma((2, 2, 6)), dma((2, 2, 6)),
             dma((1,)), dma((1,)), dma((8,)), dma((8,)),
             *[vmem((TAPS * 32, FORM), BF16)] * (NFFT // FORM),
         ],

time: 36.3 us -> 37.2 us (1.025)
  Pallas kernels: 36.2 us -> 37.1 us
    pallas_call x1, Pallas kernels: 32.4 us -> 33.2 us  [spectra_of_all(): pl.pallas_call(spectra_kernel, out_shape=[jax.ShapeDtypeStruct((512, 64),...]
where the time goes in v6:
time: 37.2 us; the launch traced here: 37.1 us
  Pallas kernels  37.1 us (100%)
    pallas_call x1, Pallas kernels, spectra_of_all(): pl.pallas_call(spectra_kernel, out_shape=[jax.ShapeDtypeStruct((512, 64),...  33.2 us
    pallas_call x1, Pallas kernels, correlate(): pl.pallas_call(correlate_kernel, out_shape=jax.ShapeDtypeStruct((2, 128,...  3.83 us

profile of v6, /device:TPU:1, one launch (start us, length us, event | category | flops | bytes accessed | tf_op | source)
XLA Modules:
  0.0 37.1 jit_solution(11806745617759470901)
XLA Ops:
  0.0 33.2 %shard_map.46 = (bf16[512,64]{1,0:T(8,128)(2,1)}, bf16[64,4096]{1,0:T(8,128)(2,1)}) custom-call(s32[16]{0:T(128)} %index_hbm.1, f32[8,8192]{1,0:T(8,128)} %taps_hbm.1, s32[16,128]{1,0:T(8,128)} %bitcast.1, bf16[16,188416]{1,0:T(8,128)(2,1)} %volts_hbm.1), custom_call_target="tpu_custom_call" | custom-call | tf_op jit(solution)/shard_map/pallas_call | solution.py:335
  33.3 3.8 %shard_map.47 = bf16[2,128,2,4096]{3,2,1,0:T(2,128)(2,1)} custom-call(bf16[512,64]{1,0:T(8,128)(2,1)} %get-tuple-element.7.lhs_hbm, bf16[64,4096]{1,0:T(8,128)(2,1)} %get-tuple-element.8.cols_hbm), custom_call_target="tpu_custom_call" | custom-call | tf_op jit(solution)/shard_map/pallas_call | solution.py:391

commit v7 on v5

--- a/solution.py
+++ b/solution.py
@@ -11,9 +11,9 @@
 F32, BF16, I32 = jnp.float32, jnp.bfloat16, jnp.int32
 MESH = pl.DeviceIdType.MESH
 NFFT, TAPS, SPEC, FRAMES = 8192, 8, 16, 23
-GROUPS = ((0, 12), (12, 11))
+GROUPS = ((0, 10), (10, 8), (18, 5))
 FORM = 1024
-QBLOCK = 1024
+QBLOCK = 2048
 PLACE = {0: 0, 1: 1, 7: 2, 2: 3, 6: 4, 3: 5, 5: 6, 4: 7}
 
 
@@ -282,10 +282,10 @@
 
     for h, d in enumerate((1, 7)):
         wait(held(yl, 1 + h), s_recv.at[d])
-        relay(h, yl, 0, (1, 3, 2))
+        relay(h, yl, 0, (1, 2, 3))
     for h, d in enumerate((1, 7)):
         wait(held(other, 1 + h), t_recv.at[d])
-        relay(h, other, 1, (3, 2))
+        relay(h, other, 1, (2, 3))
     wait(buf.at[yl, core, 0, pl.ds(0, 7)], s_recv.at[0])
     to_core(0, yl, 0, 3)
     wait(held(other, 0), t_recv.at[0])
@@ -382,8 +382,12 @@
         for c in range(2):
             x = jnp.dot(lhs[pl.ds(c * 256, 256), :], cols[:, at], preferred_element_type=F32)
             out[i, c] = x.astype(BF16).reshape(128, 2, QBLOCK)
-        pltpu.make_async_copy(out.at[i], out_hbm.at[:, :, :, at], out_sem).start()
-    pltpu.make_async_copy(out, out, out_sem).wait()
+            pltpu.make_async_copy(
+                out.at[i, c], out_hbm.at[c, :, :, at], out_sem.at[i, c]
+            ).start(priority=c)
+    for i in range(steps):
+        for c in range(2):
+            pltpu.make_async_copy(out.at[i, c], out.at[i, c], out_sem.at[i, c]).wait()
 
 
 def correlate(lhs, cols):
@@ -398,7 +402,7 @@
             vmem((512, 64), BF16),
             vmem((64, 4096), BF16),
             vmem((4096 // QBLOCK, 2, 128, 2, QBLOCK), BF16),
-            dma, dma((4096 // QBLOCK,)), dma,
+            dma, dma((4096 // QBLOCK,)), dma((4096 // QBLOCK, 2)),
         ],
         compiler_params=pltpu.CompilerParams(vmem_limit_bytes=63 << 20),
     )(lhs, cols)

time: 36.3 us -> 38.7 us (1.066)
  Pallas kernels: 36.2 us -> 38.6 us
    pallas_call x1, Pallas kernels: 32.4 us -> 35.1 us  [spectra_of_all(): pl.pallas_call(spectra_kernel, out_shape=[jax.ShapeDtypeStruct((512, 64),...]
where the time goes in v7:
time: 38.7 us; the launch traced here: 38.6 us
  Pallas kernels  38.6 us (100%)
    pallas_call x1, Pallas kernels, spectra_of_all(): pl.pallas_call(spectra_kernel, out_shape=[jax.ShapeDtypeStruct((512, 64),...  35.1 us
    pallas_call x1, Pallas kernels, correlate(): pl.pallas_call(correlate_kernel, out_shape=jax.ShapeDtypeStruct((2, 128,...  3.5 us

profile of v7, /device:TPU:1, one launch (start us, length us, event | category | flops | bytes accessed | tf_op | source)
XLA Modules:
  0.0 38.6 jit_solution(17804260533764175232)
XLA Ops:
  0.0 35.1 %shard_map.46 = (bf16[512,64]{1,0:T(8,128)(2,1)}, bf16[64,4096]{1,0:T(8,128)(2,1)}) custom-call(s32[16]{0:T(128)} %index_hbm.1, f32[8,8192]{1,0:T(8,128)} %taps_hbm.1, s32[16,128]{1,0:T(8,128)} %bitcast.1, bf16[16,188416]{1,0:T(8,128)(2,1)} %volts_hbm.1), custom_call_target="tpu_custom_call" | custom-call | tf_op jit(solution)/shard_map/pallas_call | solution.py:336
  35.1 3.5 %shard_map.47 = bf16[2,128,2,4096]{3,2,1,0:T(2,128)(2,1)} custom-call(bf16[512,64]{1,0:T(8,128)(2,1)} %get-tuple-element.7.lhs_hbm, bf16[64,4096]{1,0:T(8,128)(2,1)} %get-tuple-element.8.cols_hbm), custom_call_target="tpu_custom_call" | custom-call | tf_op jit(solution)/shard_map/pallas_call | solution.py:396

commit v8 on v7

--- a/solution.py
+++ b/solution.py
@@ -11,7 +11,7 @@
 F32, BF16, I32 = jnp.float32, jnp.bfloat16, jnp.int32
 MESH = pl.DeviceIdType.MESH
 NFFT, TAPS, SPEC, FRAMES = 8192, 8, 16, 23
-GROUPS = ((0, 10), (10, 8), (18, 5))
+GROUPS = ((0, 23),)
 FORM = 1024
 QBLOCK = 2048
 PLACE = {0: 0, 1: 1, 7: 2, 2: 3, 6: 4, 3: 5, 5: 6, 4: 7}

time: 38.7 us -> 35.1 us (0.907)
  Pallas kernels: 38.6 us -> 35 us
    pallas_call x1, Pallas kernels: 35.1 us -> 31.5 us  [spectra_of_all(): pl.pallas_call(spectra_kernel, out_shape=[jax.ShapeDtypeStruct((512, 64),...]
where the time goes in v8:
time: 35.1 us; the launch traced here: 35 us
  Pallas kernels  35 us (100%)
    pallas_call x1, Pallas kernels, spectra_of_all(): pl.pallas_call(spectra_kernel, out_shape=[jax.ShapeDtypeStruct((512, 64),...  31.5 us
    pallas_call x1, Pallas kernels, correlate(): pl.pallas_call(correlate_kernel, out_shape=jax.ShapeDtypeStruct((2, 128,...  3.5 us

profile of v8, /device:TPU:1, one launch (start us, length us, event | category | flops | bytes accessed | tf_op | source)
XLA Modules:
  0.0 35.0 jit_solution(7160864863455160508)
XLA Ops:
  0.0 31.5 %shard_map.46 = (bf16[512,64]{1,0:T(8,128)(2,1)}, bf16[64,4096]{1,0:T(8,128)(2,1)}) custom-call(s32[16]{0:T(128)} %index_hbm.1, f32[8,8192]{1,0:T(8,128)} %taps_hbm.1, s32[16,128]{1,0:T(8,128)} %bitcast.1, bf16[16,188416]{1,0:T(8,128)(2,1)} %volts_hbm.1), custom_call_target="tpu_custom_call" | custom-call | tf_op jit(solution)/shard_map/pallas_call | solution.py:336
  31.5 3.5 %shard_map.47 = bf16[2,128,2,4096]{3,2,1,0:T(2,128)(2,1)} custom-call(bf16[512,64]{1,0:T(8,128)(2,1)} %get-tuple-element.7.lhs_hbm, bf16[64,4096]{1,0:T(8,128)(2,1)} %get-tuple-element.8.cols_hbm), custom_call_target="tpu_custom_call" | custom-call | tf_op jit(solution)/shard_map/pallas_call | solution.py:396

commit v9 on v8

--- a/solution.py
+++ b/solution.py
@@ -12,7 +12,7 @@
 MESH = pl.DeviceIdType.MESH
 NFFT, TAPS, SPEC, FRAMES = 8192, 8, 16, 23
 GROUPS = ((0, 23),)
-FORM = 1024
+FORM = 2048
 QBLOCK = 2048
 PLACE = {0: 0, 1: 1, 7: 2, 2: 3, 6: 4, 3: 5, 5: 6, 4: 7}
 

time: 35.1 us -> 35.1 us (level)
  no operation moved by 1% of the time
where the time goes in v9:
time: 35.1 us; the launch traced here: 35 us
  Pallas kernels  35 us (100%)
    pallas_call x1, Pallas kernels, spectra_of_all(): pl.pallas_call(spectra_kernel, out_shape=[jax.ShapeDtypeStruct((512, 64),...  31.5 us
    pallas_call x1, Pallas kernels, correlate(): pl.pallas_call(correlate_kernel, out_shape=jax.ShapeDtypeStruct((2, 128,...  3.5 us

profile of v9, /device:TPU:1, one launch (start us, length us, event | category | flops | bytes accessed | tf_op | source)
XLA Modules:
  0.0 35.0 jit_solution(7191477736255953262)
XLA Ops:
  0.0 31.5 %shard_map.46 = (bf16[512,64]{1,0:T(8,128)(2,1)}, bf16[64,4096]{1,0:T(8,128)(2,1)}) custom-call(s32[16]{0:T(128)} %index_hbm.1, f32[8,8192]{1,0:T(8,128)} %taps_hbm.1, s32[16,128]{1,0:T(8,128)} %bitcast.1, bf16[16,188416]{1,0:T(8,128)(2,1)} %volts_hbm.1), custom_call_target="tpu_custom_call" | custom-call | tf_op jit(solution)/shard_map/pallas_call | solution.py:336
  31.5 3.5 %shard_map.47 = bf16[2,128,2,4096]{3,2,1,0:T(2,128)(2,1)} custom-call(bf16[512,64]{1,0:T(8,128)(2,1)} %get-tuple-element.7.lhs_hbm, bf16[64,4096]{1,0:T(8,128)(2,1)} %get-tuple-element.8.cols_hbm), custom_call_target="tpu_custom_call" | custom-call | tf_op jit(solution)/shard_map/pallas_call | solution.py:396
